TPU v7x, 128 devices: a whole 4x4x4 slice. The times are simulated.
128 devices in a mesh: ctx: 16 (over x, y), ch: 8 (over z, core).
Axes of the slice: x: 4, y: 4, z: 4, core: 2. Of those that a mesh axis runs over, the one named last changes fastest.
Arguments:
- inputs: bfloat16 [32768, 4096], P('ctx', 'ch'), may hold values from -6 to 6
- grad_out: bfloat16 [32768, 4096], P('ctx', 'ch'), may hold values from -6 to 6
- residues: float32 [4096, 16], P('ch'), may hold values from -4 to 4
- log_rates: float32 [4096, 16], P('ch'), may hold values from -14 to -2.99
- skip_weight: float32 [4096], P('ch'), may hold values from -4 to 4
Outputs:
- grad_inputs: bfloat16 [32768, 4096], P('ctx', 'ch')
- grad_residues: float32 [4096, 16], P('ch')
- grad_log_rates: float32 [4096, 16], P('ch')
- grad_skip_weight: float32 [4096], P('ch')
All inputs are finite; a program needn't handle non-finite values.
Results may differ from a plain program's by a relative error of at most 0.0055.
Values may be sent and summed in bfloat16 or wider, within the bound.
No kernel may reach another device: no remote copies, remote signals or barrier semaphores. Data moves between devices by JAX's collectives and lax.ppermute only.
A program may use at most 128 MiB of HBM per device.

v0:
```python
import functools
import math

import jax
import jax.numpy as jnp
import ml_dtypes
import numpy as np
from jax import lax
from jax.experimental import pallas as pl
from jax.experimental.pallas import tpu as pltpu
from jax.sharding import PartitionSpec as P

MODES = 16
BLK = 256
NODES = 24
TILE = 256
LANES = 128
GROUPS = TILE // LANES
ROWS = 8
VMEM_LIMIT = 48 * 1024 * 1024


def split_bf16(table):
    high = table.astype(ml_dtypes.bfloat16)
    low = (table - high.astype(np.float64)).astype(ml_dtypes.bfloat16)
    return high, low


@functools.cache
def tables():
    order = np.arange(NODES)
    angle = (2 * order + 1) * math.pi / (2 * NODES)
    nodes = 0.5 * BLK * (1 + np.cos(angle))
    spots = np.arange(BLK + 1.0)
    basis = ((-1.0) ** order * np.sin(angle)) / (spots[:, None] - nodes[None])
    basis = basis / basis.sum(axis=1, keepdims=True)
    ahead = basis[:BLK].T
    behind = basis[BLK - np.arange(BLK)].T
    phase = 2 * math.pi * (np.arange(BLK)[:, None] + 0.5) * np.arange(BLK)[None] / (2 * BLK)
    forward = np.concatenate([np.cos(phase), np.sin(phase)], axis=0)
    inverse = np.concatenate([np.cos(phase).T, -np.sin(phase).T], axis=1) / BLK
    bf16 = ml_dtypes.bfloat16
    trans_in = np.concatenate([forward.astype(bf16), *split_bf16(behind)], axis=0)
    trans_gr = np.concatenate([forward.astype(bf16), *split_bf16(ahead)], axis=0)
    fold = np.concatenate([ahead @ inverse, inverse[:1], np.zeros((7, 2 * BLK))], axis=0)
    fold_high, fold_low = split_bf16(fold)
    fold_table = np.concatenate([fold_high, fold_low], axis=0)
    lift_high, lift_low = split_bf16(forward @ ahead.T)
    lift_table = np.concatenate([lift_high, lift_high, lift_low], axis=1)
    spread_high, spread_low = split_bf16(behind.T)
    spread = np.concatenate([spread_high, spread_high, spread_low], axis=1)
    column = np.broadcast_to(nodes[:, None], (NODES, 128)).astype(np.float32)
    return {
        "nodes": [float(x) for x in nodes.astype(np.float32)],
        "column": column,
        "trans_in": trans_in,
        "trans_gr": trans_gr,
        "forward": forward.astype(bf16),
        "inverse": inverse.astype(bf16),
        "fold": fold_table,
        "lift": lift_table,
        "spread": spread,
    }


def dot32(left, right):
    return jnp.dot(left, right, preferred_element_type=jnp.float32)


def halves(values):
    high = values.astype(jnp.bfloat16)
    low = (values - high.astype(jnp.float32)).astype(jnp.bfloat16)
    return high, low


def sums_kernel(nodes, blocks, in_ref, gr_ref, rate_ref, tin_ref, tgr_ref, fold_ref, col_ref,
                out_ref, local_ref, uspec, gspec, mode_exp, points, cross, packed):
    log_rates = rate_ref[...].T
    rates = jnp.exp(log_rates)
    for n in range(NODES):
        mode_exp[pl.ds(n * MODES, MODES), :] = jnp.exp(rates * (-nodes[n]))
    column = col_ref[:, :1]

    def transform(b, carry):
        rows = pl.ds(pl.multiple_of(b * BLK, BLK), BLK)
        uspec[b] = dot32(tin_ref[...], in_ref[rows, :])
        gspec[b] = dot32(tgr_ref[...], gr_ref[rows, :])
        return carry

    lax.fori_loop(0, blocks, transform, 0)

    def cross_rows(j, carry):
        cos_rows = pl.ds(pl.multiple_of(j * 8, 8), 8)
        sin_rows = pl.ds(pl.multiple_of(j * 8 + BLK, 8), 8)
        real = jnp.zeros((8, TILE), jnp.float32)
        imag = jnp.zeros((8, TILE), jnp.float32)
        for b in range(blocks):
            uc, us = uspec[b, cos_rows, :], uspec[b, sin_rows, :]
            gc, gs = gspec[b, cos_rows, :], gspec[b, sin_rows, :]
            real = real + (gc * uc + gs * us)
            imag = imag + (gc * us - gs * uc)
        cross[cos_rows, :] = real
        cross[sin_rows, :] = imag
        return carry

    lax.fori_loop(0, BLK // 8, cross_rows, 0)
    high, low = halves(cross[...])
    wide = dot32(fold_ref[...], high)
    folded = wide[:32] + wide[32:] + dot32(fold_ref[:32, :], low)
    skip_row = folded[NODES:NODES + 1]

    def contract(values):
        points[0:NODES, :] = values
        points[NODES:2 * NODES, :] = values * column
        total = jnp.zeros((MODES, TILE), jnp.float32)
        moment = jnp.zeros((MODES, TILE), jnp.float32)
        for n in range(NODES):
            decay = mode_exp[pl.ds(n * MODES, MODES), :]
            total = total + decay * points[n:n + 1, :]
            moment = moment + decay * points[NODES + n:NODES + n + 1, :]
        return total, moment

    step_decay = jnp.exp(rates * (-float(BLK)))
    first, second = contract(folded[:NODES])
    zero = jnp.zeros((MODES, TILE), jnp.float32)
    top = 2 * BLK
    mid = top + NODES

    def block(b, carry):
        first, second, sum_in, mom_in, gsum, gmom, reach, offset = carry
        u_sum, u_mom = contract(uspec[b, top:mid, :] + uspec[b, mid:mid + NODES, :])
        g_sum, g_mom = contract(gspec[b, top:mid, :] + gspec[b, mid:mid + NODES, :])
        local_ref[pl.ds(pl.multiple_of(b * MODES, MODES), MODES), :] = g_sum
        first = first + g_sum * sum_in
        second = second + (g_mom * sum_in + g_sum * mom_in)
        gsum = gsum + reach * g_sum
        gmom = gmom + reach * (g_mom + offset * g_sum)
        mom_in = step_decay * (mom_in + float(BLK) * sum_in) + u_mom
        sum_in = step_decay * sum_in + u_sum
        return first, second, sum_in, mom_in, gsum, gmom, reach * step_decay, offset + float(BLK)

    first, second, sum_in, mom_in, gsum, gmom, _, _ = lax.fori_loop(
        0, blocks, block, (first, second, zero, zero, zero, zero, zero + 1.0, jnp.float32(0.0))
    )
    skip_rows = jnp.broadcast_to(skip_row, (MODES, TILE))
    parts = (first, second, sum_in, mom_in, gsum, gmom, skip_rows, rates)
    for lane in range(GROUPS):
        span = slice(lane * LANES, (lane + 1) * LANES)
        for q, part in enumerate(parts):
            packed[lane, pl.ds(q, MODES, stride=ROWS), :] = part[:, span]
        out_ref[:, span] = packed[lane]


def nearby_kernel(nodes, blocks, gr_ref, rate_ref, res_ref, skip_ref, fwd_ref, inv_ref, lift_ref,
                  near_ref, weighted_ref, impulse, filt):
    rates = jnp.exp(rate_ref[...].T)
    root = jnp.sqrt(rates)
    residues = res_ref[...].T
    weights = 0.25 * residues * root
    for n in range(NODES):
        weighted = weights * jnp.exp(rates * (-nodes[n]))
        weighted_ref[pl.ds(n * MODES, MODES), :] = weighted
        impulse[n:n + 1, :] = jnp.sum(weighted, axis=0, keepdims=True)
    high, low = halves(impulse[...])
    filt[...] = dot32(lift_ref[...], jnp.concatenate([high, low, high], axis=0))
    skip = skip_ref[...]

    def block(b, carry):
        rows = pl.ds(pl.multiple_of(b * BLK, BLK), BLK)
        grad = gr_ref[rows, :]
        spec = dot32(fwd_ref[...], grad)
        gc, gs = spec[:BLK], spec[BLK:]
        hc, hs = filt[:BLK, :], filt[BLK:, :]
        real = (gc * hc + gs * hs).astype(jnp.bfloat16)
        imag = (gc * hs - gs * hc).astype(jnp.bfloat16)
        near = dot32(inv_ref[:, :BLK], real) + dot32(inv_ref[:, BLK:], imag)
        near_ref[rows, :] = near + skip * grad.astype(jnp.float32)
        return carry

    lax.fori_loop(0, blocks, block, 0)


def scan_kernel(shards, span, in_ref, out_ref):
    decay = jnp.exp(in_ref[0, 7:8, :] * (-span))

    def row(d, q):
        return in_ref[d, q:q + 1, :]

    zero = jnp.zeros_like(decay)
    first, second, skip, sum_in, mom_in = zero, zero, zero, zero, zero
    for d in range(shards):
        gsum, gmom = row(d, 4), row(d, 5)
        first = first + (row(d, 0) + gsum * sum_in)
        second = second + (row(d, 1) + (gmom * sum_in + gsum * mom_in))
        skip = skip + row(d, 6)
        mom_in = decay * (mom_in + span * sum_in) + row(d, 3)
        sum_in = decay * sum_in + row(d, 2)
    blank = jnp.zeros((4, first.shape[1]), jnp.float32)
    back = zero
    for d in reversed(range(shards)):
        out_ref[d] = jnp.concatenate([back, first, second, skip, blank], axis=0)
        back = row(d, 4) + decay * back


def finish_kernel(blocks, scaling, near_ref, mid_ref, weighted_ref, local_ref, rate_ref, res_ref, spread_ref,
                  out_ref, gres_ref, grate_ref, gskip_ref, packed, back_scr, coef):
    rates = jnp.exp(rate_ref[...].T)
    residues = res_ref[...].T
    root = jnp.sqrt(rates)
    weights = 0.25 * residues * root
    step_decay = jnp.exp(rates * (-float(BLK)))

    for lane in range(GROUPS):
        packed[lane] = mid_ref[:, lane * LANES:(lane + 1) * LANES]

    def picked(q):
        return jnp.concatenate(
            [packed[lane, pl.ds(q, MODES, stride=ROWS), :] for lane in range(GROUPS)], axis=1
        )

    first, second = picked(1), picked(2)
    gres_ref[...] = (0.25 * root * first * scaling).T
    grate_ref[...] = ((0.125 * residues * root * first - rates * weights * second) * scaling).T
    gskip_ref[...] = mid_ref[3:4, :] * scaling
    back = picked(0)
    for b in reversed(range(blocks)):
        for lane in range(GROUPS):
            back_scr[lane, pl.ds(b, MODES, stride=blocks), :] = back[:, lane * LANES:(lane + 1) * LANES]
        back = local_ref[pl.ds(b * MODES, MODES), :] + step_decay * back
    for lane in range(GROUPS):
        span = slice(lane * LANES, (lane + 1) * LANES)
        for n in range(NODES):
            total = jnp.zeros((blocks, LANES), jnp.float32)
            for m in range(MODES):
                line = weighted_ref[n * MODES + m:n * MODES + m + 1, span]
                total = total + back_scr[lane, pl.ds(m * blocks, blocks), :] * line
            coef[lane, pl.ds(n, blocks, stride=NODES), :] = total
    for b in range(blocks):
        high, low = halves(
            jnp.concatenate([coef[lane, pl.ds(b * NODES, NODES), :] for lane in range(GROUPS)], axis=1)
        )
        far = dot32(spread_ref[...], jnp.concatenate([high, low, high], axis=0))
        rows = pl.ds(b * BLK, BLK)
        out_ref[rows, :] = (near_ref[rows, :] + far).astype(jnp.bfloat16)


def on_device(inputs, grad_out, residues, log_rates, skip_weight):
    tokens, channels = inputs.shape
    shards = lax.axis_size("ctx")
    blocks = tokens // BLK
    grid = (channels // TILE,)
    scaling = 1.0 / math.sqrt(tokens * shards)
    t = tables()
    nodes = t["nodes"]
    f32 = jnp.float32
    skip_line = skip_weight.reshape(1, channels)

    def cols(rows):
        return pl.BlockSpec((rows, TILE), lambda i: (0, i))

    per_channel = pl.BlockSpec((TILE, MODES), lambda i: (i, 0))

    def whole(table):
        return pl.BlockSpec(table.shape, lambda i: (0, 0))

    params = pltpu.CompilerParams(vmem_limit_bytes=VMEM_LIMIT)

    def cost(flops, size):
        return pl.CostEstimate(flops=int(flops), bytes_accessed=int(size), transcendentals=0)

    names = ("trans_in", "trans_gr", "fold", "column")
    consts = [jnp.asarray(t[k]) for k in names]
    spec_rows = 2 * BLK + 2 * NODES
    summed, local = pl.pallas_call(
        functools.partial(sums_kernel, nodes, blocks),
        grid=grid,
        in_specs=[cols(tokens), cols(tokens), per_channel] + [whole(c) for c in consts],
        out_specs=[cols(MODES * ROWS), cols(MODES * blocks)],
        out_shape=[
            jax.ShapeDtypeStruct((MODES * ROWS, channels), f32),
            jax.ShapeDtypeStruct((MODES * blocks, channels), f32),
        ],
        scratch_shapes=[
            pltpu.VMEM((blocks, spec_rows, TILE), f32),
            pltpu.VMEM((blocks, spec_rows, TILE), f32),
            pltpu.VMEM((NODES * MODES, TILE), f32),
            pltpu.VMEM((2 * NODES, TILE), f32),
            pltpu.VMEM((2 * BLK, TILE), f32),
            pltpu.VMEM((GROUPS, MODES * ROWS, LANES), f32),
        ],
        compiler_params=params,
        cost_estimate=cost(4 * spec_rows * tokens * channels, 8 * tokens * channels),
    )(inputs, grad_out, log_rates, *consts)

    by_mode = lax.all_to_all(
        summed.reshape(MODES, ROWS, channels), "ctx", split_axis=0, concat_axis=0, tiled=True
    )

    consts = [jnp.asarray(t[k]) for k in ("forward", "inverse", "lift")]
    nearby, weighted = pl.pallas_call(
        functools.partial(nearby_kernel, nodes, blocks),
        grid=grid,
        in_specs=[cols(tokens), per_channel, per_channel, cols(1)] + [whole(c) for c in consts],
        out_specs=[cols(tokens), cols(NODES * MODES)],
        out_shape=[
            jax.ShapeDtypeStruct((tokens, channels), f32),
            jax.ShapeDtypeStruct((NODES * MODES, channels), f32),
        ],
        scratch_shapes=[pltpu.VMEM((NODES, TILE), f32), pltpu.VMEM((2 * BLK, TILE), f32)],
        compiler_params=params,
        cost_estimate=cost(8 * BLK * tokens * channels, 6 * tokens * channels),
    )(grad_out, log_rates, residues, skip_line, *consts)

    scanned = pl.pallas_call(
        functools.partial(scan_kernel, shards, float(tokens)),
        out_shape=jax.ShapeDtypeStruct((shards, ROWS, channels), f32),
        compiler_params=params,
    )(by_mode)

    back = lax.all_to_all(scanned, "ctx", split_axis=0, concat_axis=0, tiled=True)

    spread = jnp.asarray(t["spread"])
    grad_inputs, grad_residues, grad_log_rates, grad_skip = pl.pallas_call(
        functools.partial(finish_kernel, blocks, scaling),
        grid=grid,
        in_specs=[
            cols(tokens), cols(MODES * ROWS), cols(NODES * MODES), cols(MODES * blocks),
            per_channel, per_channel, whole(spread),
        ],
        out_specs=[cols(tokens), per_channel, per_channel, cols(1)],
        out_shape=[
            jax.ShapeDtypeStruct((tokens, channels), jnp.bfloat16),
            jax.ShapeDtypeStruct((channels, MODES), f32),
            jax.ShapeDtypeStruct((channels, MODES), f32),
            jax.ShapeDtypeStruct((1, channels), f32),
        ],
        scratch_shapes=[
            pltpu.VMEM((GROUPS, MODES * ROWS, LANES), f32),
            pltpu.VMEM((GROUPS, MODES * blocks, LANES), f32),
            pltpu.VMEM((GROUPS, NODES * blocks, LANES), f32),
        ],
        compiler_params=params,
    )(nearby, back.reshape(MODES * ROWS, channels), weighted, local, log_rates, residues, spread)
    return grad_inputs, grad_residues, grad_log_rates, grad_skip.reshape(channels)


def solution(mesh):
    placed = (P("ctx", "ch"), P("ctx", "ch"), P("ch", None), P("ch", None), P("ch"))
    return jax.shard_map(
        on_device,
        mesh=mesh,
        in_specs=placed,
        out_specs=(P("ctx", "ch"), P("ch", None), P("ch", None), P("ch")),
        check_vma=False,
    )
```

profile of v0, /device:TPU:0, one launch (start us, length us, event | category | flops | bytes accessed | tf_op | source)
XLA Modules:
  0.0 57.0 jit_solution(3416825262434728279)
XLA Ops:
  0.6 0.9 %copy.17.rate_ref = f32[512,16]{1,0:T(8,128)S(1)} copy(f32[512,16]{0,1:T(8,128)} %param.16) | data formatting | bytes 65536 | tf_op args[3]
  1.5 0.0 copy-start.1
  1.5 1.6 %copy-done.1 = bf16[2048,512]{1,0:T(8,128)(2,1)S(1)} copy-done((bf16[2048,512]{1,0:T(8,128)(2,1)S(1)}, bf16[2048,512]{1,0:T(8,128)(2,1)}, u32[]{:S(2)}) %copy-start.1) | copy-done | bytes 2097176
  3.1 0.0 copy-start.2
  3.1 1.6 %copy-done.2 = bf16[2048,512]{1,0:T(8,128)(2,1)S(1)} copy-done((bf16[2048,512]{1,0:T(8,128)(2,1)S(1)}, bf16[2048,512]{1,0:T(8,128)(2,1)}, u32[]{:S(2)}) %copy-start.2) | copy-done | bytes 2097176
  4.7 0.0 copy-start.5
  4.7 1.0 %copy-done.5 = bf16[560,256]{1,0:T(8,128)(2,1)S(1)} copy-done((bf16[560,256]{1,0:T(8,128)(2,1)S(1)}, bf16[560,256]{1,0:T(8,128)(2,1)}, u32[]{:S(2)}) %copy-start.5) | copy-done | bytes 286744
  5.7 0.0 copy-start.6
  5.7 1.0 %copy-done.6 = bf16[560,256]{1,0:T(8,128)(2,1)S(1)} copy-done((bf16[560,256]{1,0:T(8,128)(2,1)S(1)}, bf16[560,256]{1,0:T(8,128)(2,1)}, u32[]{:S(2)}) %copy-start.6) | copy-done | bytes 286744
  6.6 0.0 copy-start.10
  6.6 0.8 %copy-done.10 = bf16[64,512]{1,0:T(8,128)(2,1)S(1)} copy-done((bf16[64,512]{1,0:T(8,128)(2,1)S(1)}, bf16[64,512]{1,0:T(8,128)(2,1)}, u32[]{:S(2)}) %copy-start.10) | copy-done | bytes 65560
  7.5 0.0 copy-start.11
  7.5 0.7 %copy-done.11 = f32[24,128]{1,0:T(8,128)S(1)} copy-done((f32[24,128]{1,0:T(8,128)S(1)}, f32[24,128]{1,0:T(8,128)}, u32[]{:S(2)}) %copy-start.11) | copy-done | bytes 12312
  8.2 0.0 copy-start.12
  8.2 0.0 copy-start.4
  8.2 0.0 copy-start.7
  8.2 0.0 copy-start.8
  8.2 0.0 copy-start.9
  8.2 10.5 %shard_map.157 = (f32[128,512]{1,0:T(8,128)S(1)}, f32[128,512]{1,0:T(8,128)S(1)}) custom-call(bf16[2048,512]{1,0:T(8,128)(2,1)S(1)} %copy-done.1, bf16[2048,512]{1,0:T(8,128)(2,1)S(1)} %copy-done.2, f32[512,16]{1,0:T(8,128)S(1)} %copy.17.rate_ref, bf16[560,256]{1,0:T(8,128)(2,1)S(1)} %copy-done.6, bf16[560,256]{1,0:T(8,128)(2,1)S(1)} %copy-done.5, ...), custom_call_target="tpu_custom_call" | custom-call | flops 2348810240 | bytes 8388608 | tf_op jit(solution)/shard_map/pallas_call | solution.py:274
  18.7 15.4 %all_to_all.10.in_ref = f32[16,8,512]{2,1,0:T(8,128)S(1)} all-to-all(f32[16,8,512]{2,1,0:T(8,128)S(1)} %bitcast.5), channel_id=1, replica_groups=mesh['ctx'=16,'ch'=8] {'ctx'}, dimensions={0} | all-to-all | bytes 524288 | tf_op jit(solution)/shard_map/all_to_all | solution.py:295
  34.2 0.8 %shard_map.158 = f32[16,8,512]{2,1,0:T(8,128)} custom-call(f32[16,8,512]{2,1,0:T(8,128)S(1)} %all_to_all.10.in_ref), custom_call_target="tpu_custom_call" | custom-call | tf_op jit(solution)/shard_map/pallas_call | solution.py:314
  35.0 3.6 %all-to-all-start.1 = ((f32[16,8,512]{2,1,0:T(8,128)}), f32[16,8,512]{2,1,0:T(8,128)S(1)}, u32[]{:S(2)}, u32[]{:S(2)}) async-start(f32[16,8,512]{2,1,0:T(8,128)} %shard_map.158), calls=%async_computation.1 | async-start | bytes 524288 | tf_op jit(solution)/shard_map/all_to_all | solution.py:320
  38.6 0.0 copy-done.12
  38.6 0.1 copy.18.res_ref
  38.7 0.0 copy-done.4
  38.7 0.0 copy-done.7
  38.7 0.0 copy-done.8
  38.8 0.0 copy-done.9
  38.8 0.0 copy-start.3
  38.8 1.6 %copy-done.3 = bf16[2048,512]{1,0:T(8,128)(2,1)S(1)} copy-done((bf16[2048,512]{1,0:T(8,128)(2,1)S(1)}, bf16[2048,512]{1,0:T(8,128)(2,1)}, u32[]{:S(2)}) %copy-start.3) | copy-done | bytes 2097176
  40.4 0.0 copy-start
  40.4 11.2 %shard_map.156 = (f32[2048,512]{1,0:T(8,128)}, f32[384,512]{1,0:T(8,128)S(1)}) custom-call(bf16[2048,512]{1,0:T(8,128)(2,1)S(1)} %copy-done.3, f32[512,16]{1,0:T(8,128)S(1)} %copy.17.rate_ref, f32[512,16]{1,0:T(8,128)S(1)} %copy.18.res_ref, f32[1,512]{1,0:T(1,128)S(1)} %bitcast.6, bf16[512,256]{1,0:T(8,128)(2,1)S(1)} %copy-done.8, ...), custom_call_target="tpu_custom_call" | custom-call | flops 2147483648 | bytes 6291456 | tf_op jit(solution)/shard_map/pallas_call | solution.py:300
  51.5 0.0 all-to-all-done.1
  51.5 0.0 copy-done
  51.5 4.1 %shard_map.159 = (bf16[2048,512]{1,0:T(8,128)(2,1)}, f32[512,16]{1,0:T(8,128)S(1)}, f32[512,16]{1,0:T(8,128)S(1)}, f32[1,512]{1,0:T(1,128)}) custom-call(f32[2048,512]{1,0:T(8,128)} %get-tuple-element.12.near_ref, f32[128,512]{1,0:T(8,128)S(1)} %bitcast.4, f32[384,512]{1,0:T(8,128)S(1)} %get-tuple-element.14.weighted_ref, ...), custom_call_target="tpu_custom_call" | custom-call | tf_op jit(solution)/shard_map/pallas_call | solution.py:323
  55.6 0.7 %copy.22 = f32[512,16]{0,1:T(8,128)} copy(f32[512,16]{1,0:T(8,128)S(1)} %get-tuple-element.21) | data formatting | bytes 65536
  56.3 0.7 %copy.23 = f32[512,16]{0,1:T(8,128)} copy(f32[512,16]{1,0:T(8,128)S(1)} %get-tuple-element.22) | data formatting | bytes 65536
Async XLA Ops:
  1.5 1.6 %copy-start.1 = (bf16[2048,512]{1,0:T(8,128)(2,1)S(1)}, bf16[2048,512]{1,0:T(8,128)(2,1)}, u32[]{:S(2)}) copy-start(bf16[2048,512]{1,0:T(8,128)(2,1)} %in_ref.1) | copy-start | bytes 6291460
  3.1 1.6 %copy-start.2 = (bf16[2048,512]{1,0:T(8,128)(2,1)S(1)}, bf16[2048,512]{1,0:T(8,128)(2,1)}, u32[]{:S(2)}) copy-start(bf16[2048,512]{1,0:T(8,128)(2,1)} %gr_ref.3) | copy-start | bytes 6291460
  4.7 1.0 %copy-start.5 = (bf16[560,256]{1,0:T(8,128)(2,1)S(1)}, bf16[560,256]{1,0:T(8,128)(2,1)}, u32[]{:S(2)}) copy-start(bf16[560,256]{1,0:T(8,128)(2,1)} %constant.17.clone.tgr_ref) | copy-start | bytes 860164
  5.7 1.0 %copy-start.6 = (bf16[560,256]{1,0:T(8,128)(2,1)S(1)}, bf16[560,256]{1,0:T(8,128)(2,1)}, u32[]{:S(2)}) copy-start(bf16[560,256]{1,0:T(8,128)(2,1)} %constant.16.clone.tin_ref) | copy-start | bytes 860164
  6.6 0.8 %copy-start.10 = (bf16[64,512]{1,0:T(8,128)(2,1)S(1)}, bf16[64,512]{1,0:T(8,128)(2,1)}, u32[]{:S(2)}) copy-start(bf16[64,512]{1,0:T(8,128)(2,1)} %constant.18.clone.fold_ref) | copy-start | bytes 196612
  7.5 0.7 %copy-start.11 = (f32[24,128]{1,0:T(8,128)S(1)}, f32[24,128]{1,0:T(8,128)}, u32[]{:S(2)}) copy-start(f32[24,128]{1,0:T(8,128)} %constant.19.clone.col_ref) | copy-start | bytes 36868
  8.2 30.4 %copy-start.12 = (f32[512,16]{0,1:T(8,128)S(1)}, f32[512,16]{0,1:T(8,128)}, u32[]{:S(2)}) copy-start(f32[512,16]{0,1:T(8,128)} %param.15) | copy-start | bytes 98308
  8.2 30.6 %copy-start.4 = (f32[512]{0:T(512)S(1)}, f32[512]{0:T(512)}, u32[]{:S(2)}) copy-start(f32[512]{0:T(512)} %param.17) | copy-start | bytes 6148
  8.2 30.6 %copy-start.7 = (bf16[256,512]{1,0:T(8,128)(2,1)S(1)}, bf16[256,512]{1,0:T(8,128)(2,1)}, u32[]{:S(2)}) copy-start(bf16[256,512]{1,0:T(8,128)(2,1)} %constant.21.clone.inv_ref) | copy-start | bytes 786436
  8.2 30.6 %copy-start.8 = (bf16[512,256]{1,0:T(8,128)(2,1)S(1)}, bf16[512,256]{1,0:T(8,128)(2,1)}, u32[]{:S(2)}) copy-start(bf16[512,256]{1,0:T(8,128)(2,1)} %constant.20.clone.fwd_ref) | copy-start | bytes 786436
  8.2 30.6 %copy-start.9 = (bf16[512,72]{1,0:T(8,128)(2,1)S(1)}, bf16[512,72]{1,0:T(8,128)(2,1)}, u32[]{:S(2)}) copy-start(bf16[512,72]{1,0:T(8,128)(2,1)} %constant.22.clone.lift_ref) | copy-start | bytes 221188
  35.0 16.6 %all-to-all-start.1 = ((f32[16,8,512]{2,1,0:T(8,128)}), f32[16,8,512]{2,1,0:T(8,128)S(1)}, u32[]{:S(2)}, u32[]{:S(2)}) async-start(f32[16,8,512]{2,1,0:T(8,128)} %shard_map.158), calls=%async_computation.1 | async-start | bytes 524288 | tf_op jit(solution)/shard_map/all_to_all | solution.py:320
  38.8 1.6 %copy-start.3 = (bf16[2048,512]{1,0:T(8,128)(2,1)S(1)}, bf16[2048,512]{1,0:T(8,128)(2,1)}, u32[]{:S(2)}) copy-start(bf16[2048,512]{1,0:T(8,128)(2,1)} %gr_ref.3) | copy-start | bytes 6291460
  40.4 11.2 %copy-start = (bf16[256,72]{1,0:T(8,128)(2,1)S(1)}, bf16[256,72]{1,0:T(8,128)(2,1)}, u32[]{:S(2)}) copy-start(bf16[256,72]{1,0:T(8,128)(2,1)} %constant.23.clone.spread_ref) | copy-start | bytes 110596
where the time goes:
time: 58 us; the launch traced here: 57 us
  Pallas kernels  26.6 us (46%)
  blocking collectives  15.4 us (27%)
  local copies, waits for them, and re-layouts  10.7 us (18%)
  starting transfers between devices  3.63 us (6%)
  between operations  0.74 us (1%)
    all_to_all x1, blocking collectives, on_device(): lax.all_to_all(summed.reshape(MODES, ROWS, channels), 'ctx', split_axis=0...  15.4 us
    pallas_call x1, Pallas kernels, on_device(): pl.pallas_call(functools.partial(nearby_kernel, nodes, blocks), grid=grid...  11.2 us
    unnamed x30, local copies, waits for them, and re-layouts  10.7 us
    pallas_call x1, Pallas kernels, on_device(): pl.pallas_call(functools.partial(sums_kernel, nodes, blocks), grid=grid,...  10.5 us
    pallas_call x1, Pallas kernels, on_device(): pl.pallas_call(functools.partial(finish_kernel, blocks, scaling), grid=gr...  4.08 us
    all_to_all x1, starting transfers between devices, on_device(): lax.all_to_all(scanned, 'ctx', split_axis=0, concat_axis=0, tiled=True)  3.63 us
  transfers between devices with their start and end apart: 1, of which 0 were waited for; matrix products, arithmetic and copies ran while one was open for 0% of the time, Pallas kernels for 20%

commit v1 on v0

v1 whole, which is shorter than its diff:
```python
import functools
import math

import jax
import jax.numpy as jnp
import ml_dtypes
import numpy as np
from jax import lax
from jax.experimental import pallas as pl
from jax.experimental.pallas import tpu as pltpu
from jax.sharding import PartitionSpec as P

MODES = 16
BLK = 256
NODES = 24
TILE = 256
LANES = 128
GROUPS = TILE // LANES
ROWS = 8
PAIRS = 4
VMEM_LIMIT = 24 * 1024 * 1024


def split_bf16(table):
    high = table.astype(ml_dtypes.bfloat16)
    low = (table - high.astype(np.float64)).astype(ml_dtypes.bfloat16)
    return high, low


@functools.cache
def tables():
    order = np.arange(NODES)
    angle = (2 * order + 1) * math.pi / (2 * NODES)
    nodes = 0.5 * BLK * (1 + np.cos(angle))
    spots = np.arange(BLK + 1.0)
    basis = ((-1.0) ** order * np.sin(angle)) / (spots[:, None] - nodes[None])
    basis = basis / basis.sum(axis=1, keepdims=True)
    ahead = basis[:BLK].T
    behind = basis[BLK - np.arange(BLK)].T
    phase = 2 * math.pi * (np.arange(BLK)[:, None] + 0.5) * np.arange(BLK)[None] / (2 * BLK)
    forward = np.concatenate([np.cos(phase), np.sin(phase)], axis=0)
    inverse = np.concatenate([np.cos(phase).T, -np.sin(phase).T], axis=1) / BLK
    bf16 = ml_dtypes.bfloat16
    trans_in = np.concatenate([forward.astype(bf16), *split_bf16(behind)], axis=0)
    trans_gr = np.concatenate([forward.astype(bf16), *split_bf16(ahead)], axis=0)
    fold = np.concatenate([ahead @ inverse, inverse[:1], np.zeros((7, 2 * BLK))], axis=0)
    fold_high, fold_low = split_bf16(fold)
    fold_table = np.concatenate([fold_high, fold_low], axis=0)
    lift_high, lift_low = split_bf16(forward @ ahead.T)
    lift_table = np.concatenate([lift_high, lift_high, lift_low], axis=1)
    spread_high, spread_low = split_bf16(behind.T)
    spread = np.concatenate([spread_high, spread_high, spread_low], axis=1)
    return {
        "nodes": [float(x) for x in nodes.astype(np.float32)],
        "trans_in": trans_in,
        "trans_gr": trans_gr,
        "forward": forward.astype(bf16),
        "inverse": inverse.astype(bf16),
        "fold": fold_table,
        "lift": lift_table,
        "spread": spread,
    }


def dot32(left, right):
    return jnp.dot(left, right, preferred_element_type=jnp.float32)


def halves(values):
    high = values.astype(jnp.bfloat16)
    low = (values - high.astype(jnp.float32)).astype(jnp.bfloat16)
    return high, low


def sums_kernel(nodes, blocks, in_hbm, gr_hbm, rate_hbm, tin_hbm, tgr_hbm, fold_hbm,
                out_ref, local_ref, rate_ref, in_ref, gr_ref, tin_ref, tgr_ref, fold_ref, uspec, gspec,
                mode_exp, points, cross, packed, table_sem, in_sem, gr_sem):
    channels = rate_ref.shape[1]
    tiles = channels // TILE
    spec_rows = 2 * BLK + 2 * NODES

    def tables_in():
        return [
            pltpu.make_async_copy(src, dst, table_sem.at[k])
            for k, (src, dst) in enumerate(((tin_hbm, tin_ref), (tgr_hbm, tgr_ref), (fold_hbm, fold_ref)))
        ]

    def block_in(b):
        rows = pl.ds(b * BLK, BLK)
        return (
            pltpu.make_async_copy(in_hbm.at[rows, :], in_ref.at[rows, :], in_sem.at[b]),
            pltpu.make_async_copy(gr_hbm.at[rows, :], gr_ref.at[rows, :], gr_sem.at[b]),
        )

    rate_copy = pltpu.make_async_copy(rate_hbm, rate_ref, table_sem.at[3])
    rate_copy.start()
    table_copies = tables_in()
    table_copies[0].start()
    block_copies = [block_in(b) for b in range(blocks)]
    block_copies[0][0].start()
    table_copies[1].start()
    block_copies[0][1].start()
    for b in range(1, blocks):
        block_copies[b][0].start()
        block_copies[b][1].start()
    table_copies[2].start()

    rate_copy.wait()
    rates = jnp.exp(rate_ref[...])
    step_decay = jnp.exp(rates * (-float(BLK)))
    for n in range(NODES):
        mode_exp[pl.ds(n * MODES, MODES), :] = jnp.exp(rates * (-nodes[n]))

    def lanes(c):
        return slice(c * TILE, (c + 1) * TILE)

    def transform(b):
        slot = b % PAIRS
        rows = slice(b * BLK, (b + 1) * BLK)

        def product(spec, table, data, c):
            def emit():
                spec[slot, :, lanes(c)] = dot32(table[...], data[rows, lanes(c)])

            return emit

        return [
            product(spec, table, data, c)
            for c in range(tiles)
            for spec, table, data in ((uspec, tin_ref, in_ref), (gspec, tgr_ref, gr_ref))
        ]

    def cross_rows(first_block, c, low, high):
        def emit():
            for j in range(low, high):
                cos_rows = slice(j * 8, j * 8 + 8)
                sin_rows = slice(BLK + j * 8, BLK + j * 8 + 8)
                real, imag = None, None
                for b in (first_block, first_block + 1):
                    slot = b % PAIRS
                    uc, us = uspec[slot, cos_rows, lanes(c)], uspec[slot, sin_rows, lanes(c)]
                    gc, gs = gspec[slot, cos_rows, lanes(c)], gspec[slot, sin_rows, lanes(c)]
                    re, im = gc * uc + gs * us, gc * us - gs * uc
                    real = re if real is None else real + re
                    imag = im if imag is None else imag + im
                if first_block:
                    real = real + cross[cos_rows, lanes(c)]
                    imag = imag + cross[sin_rows, lanes(c)]
                cross[cos_rows, lanes(c)] = real
                cross[sin_rows, lanes(c)] = imag

        return emit

    def contract(c, series):
        count = len(series)
        for k, values in enumerate(series):
            points[c, k] = values
        zero = jnp.zeros((MODES, TILE), jnp.float32)
        totals, moments = [zero] * count, [zero] * count
        for n in range(NODES):
            decay = mode_exp[n * MODES:(n + 1) * MODES, lanes(c)]
            scaled = decay * nodes[n]
            for k in range(count):
                line = points[c, k, n:n + 1, :]
                totals[k] = totals[k] + decay * line
                moments[k] = moments[k] + scaled * line
        return totals, moments

    top = 2 * BLK
    mid = top + NODES
    zero = jnp.zeros((MODES, TILE), jnp.float32)
    state = [[zero, zero, zero, zero, zero, zero, zero + 1.0] for _ in range(tiles)]

    def modal_pair(first_block, c):
        def emit():
            first, second, sum_in, mom_in, gsum, gmom, reach = state[c]
            series = []
            for b in (first_block, first_block + 1):
                for spec in (uspec, gspec):
                    slot = b % PAIRS
                    series.append(spec[slot, top:mid, lanes(c)] + spec[slot, mid:spec_rows, lanes(c)])
            totals, moments = contract(c, series)
            decay = step_decay[:, lanes(c)]
            for k in range(2):
                b = first_block + k
                u_sum, g_sum = totals[2 * k], totals[2 * k + 1]
                u_mom, g_mom = moments[2 * k], moments[2 * k + 1]
                local_ref[b * MODES:(b + 1) * MODES, lanes(c)] = g_sum
                first = first + g_sum * sum_in
                second = second + (g_mom * sum_in + g_sum * mom_in)
                gsum = gsum + reach * g_sum
                gmom = gmom + reach * (g_mom + float(BLK * b) * g_sum)
                mom_in = decay * (mom_in + float(BLK) * sum_in) + u_mom
                sum_in = decay * sum_in + u_sum
                reach = reach * decay
            state[c] = [first, second, sum_in, mom_in, gsum, gmom, reach]

        return emit

    table_copies[0].wait()
    table_copies[1].wait()
    def pair_work(first_block):
        work = []
        for c in range(tiles):
            work.append(cross_rows(first_block, c, 0, BLK // 16))
            work.append(modal_pair(first_block, c))
            work.append(cross_rows(first_block, c, BLK // 16, BLK // 8))
        return work

    for pair in range(0, blocks, 2):
        for b in (pair, pair + 1):
            for copy in block_copies[b]:
                copy.wait()
        products = transform(pair) + transform(pair + 1)
        work = pair_work(pair - 2) if pair else []
        for k, product in enumerate(products):
            product()
            if k < len(work):
                work[k]()
    for emit in pair_work(blocks - 2):
        emit()
    table_copies[2].wait()
    for c in range(tiles):
        high, low = halves(cross[:, lanes(c)])
        wide = dot32(fold_ref[...], high)
        folded = wide[:32] + wide[32:] + dot32(fold_ref[:32, :], low)
        totals, moments = contract(c, [folded[:NODES]])
        first, second, sum_in, mom_in, gsum, gmom, _ = state[c]
        skip_rows = jnp.broadcast_to(folded[NODES:NODES + 1], (MODES, TILE))
        parts = (first + totals[0], second + moments[0], sum_in, mom_in, gsum, gmom, skip_rows, rates[:, lanes(c)])
        for half in range(GROUPS):
            span = slice(half * LANES, (half + 1) * LANES)
            group = c * GROUPS + half
            for q, part in enumerate(parts):
                packed[group, pl.ds(q, MODES, stride=ROWS), :] = part[:, span]
            out_ref[:, group * LANES:(group + 1) * LANES] = packed[group]


def nearby_kernel(nodes, blocks, gr_ref, rate_ref, res_ref, skip_ref, fwd_ref, inv_ref, lift_ref,
                  near_ref, weighted_ref, impulse, filt):
    rates = jnp.exp(rate_ref[...])
    root = jnp.sqrt(rates)
    residues = res_ref[...]
    weights = 0.25 * residues * root
    for n in range(NODES):
        weighted = weights * jnp.exp(rates * (-nodes[n]))
        weighted_ref[pl.ds(n * MODES, MODES), :] = weighted
        impulse[n:n + 1, :] = jnp.sum(weighted, axis=0, keepdims=True)
    high, low = halves(impulse[...])
    filt[...] = dot32(lift_ref[...], jnp.concatenate([high, low, high], axis=0))
    skip = skip_ref[...]

    for b in range(blocks):
        rows = slice(b * BLK, (b + 1) * BLK)
        grad = gr_ref[rows, :]
        spec = dot32(fwd_ref[...], grad)
        gc, gs = spec[:BLK], spec[BLK:]
        hc, hs = filt[:BLK, :], filt[BLK:, :]
        real = (gc * hc + gs * hs).astype(jnp.bfloat16)
        imag = (gc * hs - gs * hc).astype(jnp.bfloat16)
        near = dot32(inv_ref[:, :BLK], real) + dot32(inv_ref[:, BLK:], imag)
        near_ref[rows, :] = near + skip * grad.astype(jnp.float32)


def scan_kernel(shards, span, in_ref, out_ref):
    decay = jnp.exp(in_ref[0, 7:8, :] * (-span))

    def row(d, q):
        return in_ref[d, q:q + 1, :]

    zero = jnp.zeros_like(decay)
    first, second, skip, sum_in, mom_in = zero, zero, zero, zero, zero
    for d in range(shards):
        gsum, gmom = row(d, 4), row(d, 5)
        first = first + (row(d, 0) + gsum * sum_in)
        second = second + (row(d, 1) + (gmom * sum_in + gsum * mom_in))
        skip = skip + row(d, 6)
        mom_in = decay * (mom_in + span * sum_in) + row(d, 3)
        sum_in = decay * sum_in + row(d, 2)
    blank = jnp.zeros((4, first.shape[1]), jnp.float32)
    back = zero
    for d in reversed(range(shards)):
        out_ref[d] = jnp.concatenate([back, first, second, skip, blank], axis=0)
        back = row(d, 4) + decay * back


def finish_kernel(blocks, scaling, near_hbm, mid_ref, weighted_ref, local_ref, rate_ref, res_ref, spread_ref,
                  out_hbm, gres_ref, grate_ref, gskip_ref, near_ref, out_ref, packed, back_scr, coef,
                  near_sem, out_sem):
    channels = rate_ref.shape[1]
    groups = channels // LANES

    def near_in(b):
        rows = pl.ds(b * BLK, BLK)
        return pltpu.make_async_copy(near_hbm.at[rows, :], near_ref.at[rows, :], near_sem.at[b])

    def block_out(b):
        rows = pl.ds(b * BLK, BLK)
        return pltpu.make_async_copy(out_ref.at[rows, :], out_hbm.at[rows, :], out_sem.at[b])

    for b in range(blocks):
        near_in(b).start()

    rates = jnp.exp(rate_ref[...])
    residues = res_ref[...]
    root = jnp.sqrt(rates)
    weights = 0.25 * residues * root
    step_decay = jnp.exp(rates * (-float(BLK)))
    for lane in range(groups):
        packed[lane] = mid_ref[:, lane * LANES:(lane + 1) * LANES]

    def picked(q):
        return jnp.concatenate(
            [packed[lane, pl.ds(q, MODES, stride=ROWS), :] for lane in range(groups)], axis=1
        )

    back = picked(0)
    for b in reversed(range(blocks)):
        for lane in range(groups):
            back_scr[lane, pl.ds(b, MODES, stride=blocks), :] = back[:, lane * LANES:(lane + 1) * LANES]
        back = local_ref[b * MODES:(b + 1) * MODES, :] + step_decay * back
    for lane in range(groups):
        span = slice(lane * LANES, (lane + 1) * LANES)
        for n in range(NODES):
            total = jnp.zeros((blocks, LANES), jnp.float32)
            for m in range(MODES):
                line = weighted_ref[n * MODES + m:n * MODES + m + 1, span]
                total = total + back_scr[lane, m * blocks:(m + 1) * blocks, :] * line
            coef[lane, pl.ds(n, blocks, stride=NODES), :] = total
    for b in range(blocks):
        high, low = halves(
            jnp.concatenate([coef[lane, b * NODES:(b + 1) * NODES, :] for lane in range(groups)], axis=1)
        )
        far = dot32(spread_ref[...], jnp.concatenate([high, low, high], axis=0))
        rows = slice(b * BLK, (b + 1) * BLK)
        near_in(b).wait()
        out_ref[rows, :] = (near_ref[rows, :] + far).astype(jnp.bfloat16)
        block_out(b).start()
    first, second = picked(1), picked(2)
    gres_ref[...] = 0.25 * root * first * scaling
    grate_ref[...] = (0.125 * residues * root * first - rates * weights * second) * scaling
    gskip_ref[...] = mid_ref[3:4, :] * scaling
    for b in range(blocks):
        block_out(b).wait()


def cols(rows):
    return pl.BlockSpec((rows, TILE), lambda i: (0, i))


def whole(table):
    return pl.BlockSpec(table.shape, lambda i: (0, 0))


def f32_rows(rows, channels):
    return jax.ShapeDtypeStruct((rows, channels), jnp.float32)


def cost(flops, size):
    return pl.CostEstimate(flops=int(flops), bytes_accessed=int(size), transcendentals=0)


PARAMS = pltpu.CompilerParams(vmem_limit_bytes=VMEM_LIMIT)


def call_sums(inputs, grad_out, log_rates):
    tokens, channels = inputs.shape
    blocks = tokens // BLK
    t = tables()
    consts = [jnp.asarray(t[k]) for k in ("trans_in", "trans_gr", "fold")]
    spec_rows = 2 * BLK + 2 * NODES
    far = pl.BlockSpec(memory_space=pltpu.HBM)
    near = pl.BlockSpec(memory_space=pltpu.VMEM)
    return pl.pallas_call(
        functools.partial(sums_kernel, t["nodes"], blocks),
        in_specs=[far] * 6,
        out_specs=[near, near],
        out_shape=[f32_rows(MODES * ROWS, channels), f32_rows(MODES * blocks, channels)],
        scratch_shapes=[
            pltpu.VMEM((MODES, channels), jnp.float32),
            pltpu.VMEM((tokens, channels), jnp.bfloat16),
            pltpu.VMEM((tokens, channels), jnp.bfloat16),
            pltpu.VMEM(consts[0].shape, jnp.bfloat16),
            pltpu.VMEM(consts[1].shape, jnp.bfloat16),
            pltpu.VMEM(consts[2].shape, jnp.bfloat16),
            pltpu.VMEM((PAIRS, spec_rows, channels), jnp.float32),
            pltpu.VMEM((PAIRS, spec_rows, channels), jnp.float32),
            pltpu.VMEM((NODES * MODES, channels), jnp.float32),
            pltpu.VMEM((channels // TILE, 4, NODES, TILE), jnp.float32),
            pltpu.VMEM((2 * BLK, channels), jnp.float32),
            pltpu.VMEM((channels // LANES, MODES * ROWS, LANES), jnp.float32),
            pltpu.SemaphoreType.DMA((4,)),
            pltpu.SemaphoreType.DMA((blocks,)),
            pltpu.SemaphoreType.DMA((blocks,)),
        ],
        compiler_params=PARAMS,
        cost_estimate=cost(4 * spec_rows * tokens * channels, 8 * tokens * channels),
    )(*(pltpu.with_memory_space_constraint(x, pltpu.HBM) for x in (inputs, grad_out, log_rates, *consts)))


def call_nearby(grad_out, log_rates, residues, skip_line):
    tokens, channels = grad_out.shape
    t = tables()
    consts = [jnp.asarray(t[k]) for k in ("forward", "inverse", "lift")]
    return pl.pallas_call(
        functools.partial(nearby_kernel, t["nodes"], tokens // BLK),
        grid=(channels // TILE,),
        in_specs=[cols(tokens), cols(MODES), cols(MODES), cols(1)] + [whole(c) for c in consts],
        out_specs=[cols(tokens), cols(NODES * MODES)],
        out_shape=[f32_rows(tokens, channels), f32_rows(NODES * MODES, channels)],
        scratch_shapes=[pltpu.VMEM((NODES, TILE), jnp.float32), pltpu.VMEM((2 * BLK, TILE), jnp.float32)],
        compiler_params=PARAMS,
        cost_estimate=cost(8 * BLK * tokens * channels, 6 * tokens * channels),
    )(grad_out, log_rates, residues, skip_line, *consts)


def call_scan(by_mode, tokens):
    return pl.pallas_call(
        functools.partial(scan_kernel, by_mode.shape[0], float(tokens)),
        out_shape=jax.ShapeDtypeStruct(by_mode.shape, jnp.float32),
        compiler_params=PARAMS,
    )(by_mode)


def call_finish(scaling, nearby, back, weighted, local, log_rates, residues):
    tokens, channels = nearby.shape
    blocks = tokens // BLK
    spread = jnp.asarray(tables()["spread"])
    far = pl.BlockSpec(memory_space=pltpu.HBM)
    near = pl.BlockSpec(memory_space=pltpu.VMEM)
    return pl.pallas_call(
        functools.partial(finish_kernel, blocks, scaling),
        in_specs=[far] + [near] * 6,
        out_specs=[far, near, near, near],
        out_shape=[
            jax.ShapeDtypeStruct((tokens, channels), jnp.bfloat16),
            f32_rows(MODES, channels),
            f32_rows(MODES, channels),
            f32_rows(1, channels),
        ],
        scratch_shapes=[
            pltpu.VMEM((tokens, channels), nearby.dtype),
            pltpu.VMEM((tokens, channels), jnp.bfloat16),
            pltpu.VMEM((channels // LANES, MODES * ROWS, LANES), jnp.float32),
            pltpu.VMEM((channels // LANES, MODES * blocks, LANES), jnp.float32),
            pltpu.VMEM((channels // LANES, NODES * blocks, LANES), jnp.float32),
            pltpu.SemaphoreType.DMA((blocks,)),
            pltpu.SemaphoreType.DMA((blocks,)),
        ],
        compiler_params=PARAMS,
    )(pltpu.with_memory_space_constraint(nearby, pltpu.HBM), back, weighted, local, log_rates, residues, spread)


def on_device(inputs, grad_out, residues, log_rates, skip_weight):
    tokens, channels = inputs.shape
    scaling = 1.0 / math.sqrt(tokens * lax.axis_size("ctx"))
    residues, log_rates = residues.T, log_rates.T
    summed, local = call_sums(inputs, grad_out, log_rates)
    by_mode = lax.all_to_all(
        summed.reshape(MODES, ROWS, channels), "ctx", split_axis=0, concat_axis=0, tiled=True
    )
    nearby, weighted = call_nearby(grad_out, log_rates, residues, skip_weight.reshape(1, channels))
    scanned = call_scan(by_mode, tokens)
    back = lax.all_to_all(scanned, "ctx", split_axis=0, concat_axis=0, tiled=True)
    grad_inputs, grad_residues, grad_log_rates, grad_skip = call_finish(
        scaling, nearby, back.reshape(MODES * ROWS, channels), weighted, local, log_rates, residues
    )
    return grad_inputs, grad_residues.T, grad_log_rates.T, grad_skip.reshape(channels)


def solution(mesh):
    placed = (P("ctx", "ch"), P("ctx", "ch"), P("ch", None), P("ch", None), P("ch"))
    return jax.shard_map(
        on_device,
        mesh=mesh,
        in_specs=placed,
        out_specs=(P("ctx", "ch"), P("ch", None), P("ch", None), P("ch")),
        check_vma=False,
    )
```

time: 58 us -> 42.2 us (0.73)
  Pallas kernels: 26.6 us -> 17 us
  local copies, waits for them, and re-layouts: 10.7 us -> 4.76 us
    pallas_call x4, Pallas kernels: 26.6 us -> 17 us  [the longest x1 7.78 us: call_sums(): pl.pallas_call(functools.partial(sums_kernel, t['nodes'], blocks), in_spe...]
    unnamed x30 -> x18, local copies, waits for them, and re-layouts: 10.7 us -> 4.76 us
  transfers between devices with their start and end apart: 1 -> 1, of which waited for: 0 -> 0; matrix products, arithmetic and copies ran while one was open for 0% -> 0% of each run, Pallas kernels for 20% -> 10%
where the time goes in v1:
time: 42.2 us; the launch traced here: 41.6 us
  Pallas kernels  17 us (40%)
  blocking collectives  15.4 us (36%)
  local copies, waits for them, and re-layouts  4.76 us (11%)
  starting transfers between devices  3.63 us (9%)
  between operations  0.74 us (2%)
    all_to_all x1, blocking collectives, on_device(): lax.all_to_all(summed.reshape(MODES, ROWS, channels), 'ctx', split_axis=0...  15.4 us
    pallas_call x1, Pallas kernels, call_sums(): pl.pallas_call(functools.partial(sums_kernel, t['nodes'], blocks), in_spe...  7.78 us
    unnamed x18, local copies, waits for them, and re-layouts  4.76 us
    pallas_call x1, Pallas kernels, call_nearby(): pl.pallas_call(functools.partial(nearby_kernel, t['nodes'], tokens // BLK...  4.26 us
    pallas_call x1, Pallas kernels, call_finish(): pl.pallas_call(functools.partial(finish_kernel, blocks, scaling), in_spec...  4.15 us
    all_to_all x1, starting transfers between devices, on_device(): lax.all_to_all(scanned, 'ctx', split_axis=0, concat_axis=0, tiled=True)  3.63 us
  transfers between devices with their start and end apart: 1, of which 0 were waited for; matrix products, arithmetic and copies ran while one was open for 0% of the time, Pallas kernels for 10%

profile of v1, /device:TPU:0, one launch (start us, length us, event | category | flops | bytes accessed | tf_op | source)
XLA Modules:
  0.0 41.6 jit_solution(6886224966934887346)
XLA Ops:
  0.6 0.0 copy-start.2
  0.6 0.0 copy-start.3
  0.7 0.0 copy-start.4
  0.7 0.0 copy-start.5
  0.7 7.8 %shard_map.148 = (f32[128,512]{1,0:T(8,128)S(1)}, f32[128,512]{1,0:T(8,128)S(1)}) custom-call(bf16[2048,512]{1,0:T(8,128)(2,1)} %in_hbm.1, bf16[2048,512]{1,0:T(8,128)(2,1)} %gr_hbm.1, f32[16,512]{1,0:T(8,128)} %bitcast.10, bf16[560,256]{1,0:T(8,128)(2,1)} %constant.14.clone.tin_hbm, bf16[560,256]{1,0:T(8,128)(2,1)} %constant.15.clone.tgr_hbm, ...), custom_call_target="tpu_custom_call" | custom-call | flops 2348810240 | bytes 8388608 | tf_op jit(solution)/shard_map/pallas_call | solution.py:374
  8.5 15.4 %all_to_all.10.in_ref = f32[16,8,512]{2,1,0:T(8,128)S(1)} all-to-all(f32[16,8,512]{2,1,0:T(8,128)S(1)} %bitcast.9), channel_id=1, replica_groups=mesh['ctx'=16,'ch'=8] {'ctx'}, dimensions={0} | all-to-all | bytes 524288 | tf_op jit(solution)/shard_map/all_to_all | solution.py:459
  23.9 0.8 %shard_map.149 = f32[16,8,512]{2,1,0:T(8,128)} custom-call(f32[16,8,512]{2,1,0:T(8,128)S(1)} %all_to_all.10.in_ref), custom_call_target="tpu_custom_call" | custom-call | tf_op jit(solution)/shard_map/pallas_call | solution.py:418
  24.7 3.6 %all-to-all-start.1 = ((f32[16,8,512]{2,1,0:T(8,128)}), f32[16,8,512]{2,1,0:T(8,128)S(1)}, u32[]{:S(2)}, u32[]{:S(2)}) async-start(f32[16,8,512]{2,1,0:T(8,128)} %shard_map.149), calls=%async_computation.1 | async-start | bytes 524288 | tf_op jit(solution)/shard_map/all_to_all | solution.py:464
  28.3 0.0 copy-done.2
  28.3 0.0 copy-done.3
  28.4 0.0 copy-done.4
  28.4 0.0 copy-done.5
  28.4 0.0 copy-start.6
  28.4 0.9 %copy-done.6 = bf16[256,512]{1,0:T(8,128)(2,1)S(1)} copy-done((bf16[256,512]{1,0:T(8,128)(2,1)S(1)}, bf16[256,512]{1,0:T(8,128)(2,1)}, u32[]{:S(2)}) %copy-start.6) | copy-done | bytes 262168
  29.3 0.0 copy-start.7
  29.3 0.9 %copy-done.7 = bf16[512,256]{1,0:T(8,128)(2,1)S(1)} copy-done((bf16[512,256]{1,0:T(8,128)(2,1)S(1)}, bf16[512,256]{1,0:T(8,128)(2,1)}, u32[]{:S(2)}) %copy-start.7) | copy-done | bytes 262168
  30.3 0.0 copy-start.8
  30.3 0.9 %copy-done.8 = bf16[512,72]{1,0:T(8,128)(2,1)S(1)} copy-done((bf16[512,72]{1,0:T(8,128)(2,1)S(1)}, bf16[512,72]{1,0:T(8,128)(2,1)}, u32[]{:S(2)}) %copy-start.8) | copy-done | bytes 73752
  31.2 0.0 copy-start.1
  31.2 4.3 %shard_map.147 = (f32[2048,512]{1,0:T(8,128)S(1)}, f32[384,512]{1,0:T(8,128)S(1)}) custom-call(bf16[2048,512]{1,0:T(8,128)(2,1)S(1)} %copy-done.4, f32[16,512]{1,0:T(8,128)S(1)} %bitcast.11, f32[16,512]{1,0:T(8,128)S(1)} %bitcast.13, f32[1,512]{1,0:T(1,128)S(1)} %bitcast.15, bf16[512,256]{1,0:T(8,128)(2,1)S(1)} %copy-done.7, bf16[256,512]{1,0:T(8,128)(2,1)S(1)} %copy-done.6, ...), custom_call_target="tpu_custom_call" | custom-call | flops 2147483648 | bytes 6291456 | tf_op jit(solution)/shard_map/pallas_call | solution.py:405
  35.5 0.0 copy-start
  35.5 1.9 %copy-done = f32[2048,512]{1,0:T(8,128)} copy-done((f32[2048,512]{1,0:T(8,128)}, f32[2048,512]{1,0:T(8,128)S(1)}, u32[]{:S(2)}) %copy-start) | copy-done | bytes 4194328
  37.4 0.0 all-to-all-done.1
  37.4 0.0 copy-done.1
  37.4 4.2 %shard_map.150 = (bf16[2048,512]{1,0:T(8,128)(2,1)}, f32[16,512]{1,0:T(8,128)}, f32[16,512]{1,0:T(8,128)}, f32[1,512]{1,0:T(1,128)}) custom-call(f32[2048,512]{1,0:T(8,128)} %copy-done, f32[128,512]{1,0:T(8,128)S(1)} %bitcast.8, f32[384,512]{1,0:T(8,128)S(1)} %get-tuple-element.14.weighted_ref, f32[128,512]{1,0:T(8,128)S(1)} %get-tuple-element.15.local_ref, ...), custom_call_target="tpu_custom_call" | custom-call | tf_op jit(solution)/shard_map/pallas_call | solution.py:431
Async XLA Ops:
  0.6 27.7 %copy-start.2 = (f32[512,16]{0,1:T(8,128)S(1)}, f32[512,16]{0,1:T(8,128)}, u32[]{:S(2)}) copy-start(f32[512,16]{0,1:T(8,128)} %param.15) | copy-start | bytes 98308
  0.6 27.7 %copy-start.3 = (f32[512,16]{0,1:T(8,128)S(1)}, f32[512,16]{0,1:T(8,128)}, u32[]{:S(2)}) copy-start(f32[512,16]{0,1:T(8,128)} %param.14) | copy-start | bytes 98308
  0.7 27.7 %copy-start.4 = (bf16[2048,512]{1,0:T(8,128)(2,1)S(1)}, bf16[2048,512]{1,0:T(8,128)(2,1)}, u32[]{:S(2)}) copy-start(bf16[2048,512]{1,0:T(8,128)(2,1)} %gr_hbm.1) | copy-start | bytes 6291460
  0.7 27.7 %copy-start.5 = (f32[512]{0:T(512)S(1)}, f32[512]{0:T(512)}, u32[]{:S(2)}) copy-start(f32[512]{0:T(512)} %param.16) | copy-start | bytes 6148
  24.7 12.7 %all-to-all-start.1 = ((f32[16,8,512]{2,1,0:T(8,128)}), f32[16,8,512]{2,1,0:T(8,128)S(1)}, u32[]{:S(2)}, u32[]{:S(2)}) async-start(f32[16,8,512]{2,1,0:T(8,128)} %shard_map.149), calls=%async_computation.1 | async-start | bytes 524288 | tf_op jit(solution)/shard_map/all_to_all | solution.py:464
  28.4 1.0 %copy-start.6 = (bf16[256,512]{1,0:T(8,128)(2,1)S(1)}, bf16[256,512]{1,0:T(8,128)(2,1)}, u32[]{:S(2)}) copy-start(bf16[256,512]{1,0:T(8,128)(2,1)} %constant.18.clone.inv_ref) | copy-start | bytes 786436
  29.3 0.9 %copy-start.7 = (bf16[512,256]{1,0:T(8,128)(2,1)S(1)}, bf16[512,256]{1,0:T(8,128)(2,1)}, u32[]{:S(2)}) copy-start(bf16[512,256]{1,0:T(8,128)(2,1)} %constant.17.clone.fwd_ref) | copy-start | bytes 786436
  30.3 0.9 %copy-start.8 = (bf16[512,72]{1,0:T(8,128)(2,1)S(1)}, bf16[512,72]{1,0:T(8,128)(2,1)}, u32[]{:S(2)}) copy-start(bf16[512,72]{1,0:T(8,128)(2,1)} %constant.19.clone.lift_ref) | copy-start | bytes 221188
  31.2 6.2 %copy-start.1 = (bf16[256,72]{1,0:T(8,128)(2,1)S(1)}, bf16[256,72]{1,0:T(8,128)(2,1)}, u32[]{:S(2)}) copy-start(bf16[256,72]{1,0:T(8,128)(2,1)} %constant.20.clone.spread_ref) | copy-start | bytes 110596
  35.5 1.9 %copy-start = (f32[2048,512]{1,0:T(8,128)}, f32[2048,512]{1,0:T(8,128)S(1)}, u32[]{:S(2)}) copy-start(f32[2048,512]{1,0:T(8,128)S(1)} %get-tuple-element.12.near_hbm) | copy-start | bytes 12582916

commit v2 on v1

--- a/solution.py
+++ b/solution.py
@@ -18,6 +18,8 @@
 GROUPS = TILE // LANES
 ROWS = 8
 PAIRS = 4
+SCHEDULE = ((0, 1), (2, 3), (4, 5), (6,), (7,))
+NEAR_TYPE = jnp.bfloat16
 VMEM_LIMIT = 24 * 1024 * 1024
 
 
@@ -130,20 +132,20 @@
             for spec, table, data in ((uspec, tin_ref, in_ref), (gspec, tgr_ref, gr_ref))
         ]
 
-    def cross_rows(first_block, c, low, high):
+    def cross_rows(group, c, low, high):
         def emit():
             for j in range(low, high):
                 cos_rows = slice(j * 8, j * 8 + 8)
                 sin_rows = slice(BLK + j * 8, BLK + j * 8 + 8)
                 real, imag = None, None
-                for b in (first_block, first_block + 1):
+                for b in group:
                     slot = b % PAIRS
                     uc, us = uspec[slot, cos_rows, lanes(c)], uspec[slot, sin_rows, lanes(c)]
                     gc, gs = gspec[slot, cos_rows, lanes(c)], gspec[slot, sin_rows, lanes(c)]
                     re, im = gc * uc + gs * us, gc * us - gs * uc
                     real = re if real is None else real + re
                     imag = im if imag is None else imag + im
-                if first_block:
+                if group[0]:
                     real = real + cross[cos_rows, lanes(c)]
                     imag = imag + cross[sin_rows, lanes(c)]
                 cross[cos_rows, lanes(c)] = real
@@ -171,18 +173,17 @@
     zero = jnp.zeros((MODES, TILE), jnp.float32)
     state = [[zero, zero, zero, zero, zero, zero, zero + 1.0] for _ in range(tiles)]
 
-    def modal_pair(first_block, c):
+    def modal(group, c):
         def emit():
             first, second, sum_in, mom_in, gsum, gmom, reach = state[c]
             series = []
-            for b in (first_block, first_block + 1):
+            for b in group:
                 for spec in (uspec, gspec):
                     slot = b % PAIRS
                     series.append(spec[slot, top:mid, lanes(c)] + spec[slot, mid:spec_rows, lanes(c)])
             totals, moments = contract(c, series)
             decay = step_decay[:, lanes(c)]
-            for k in range(2):
-                b = first_block + k
+            for k, b in enumerate(group):
                 u_sum, g_sum = totals[2 * k], totals[2 * k + 1]
                 u_mom, g_mom = moments[2 * k], moments[2 * k + 1]
                 local_ref[b * MODES:(b + 1) * MODES, lanes(c)] = g_sum
@@ -199,25 +200,31 @@
 
     table_copies[0].wait()
     table_copies[1].wait()
-    def pair_work(first_block):
+    def vector_work(group):
         work = []
         for c in range(tiles):
-            work.append(cross_rows(first_block, c, 0, BLK // 16))
-            work.append(modal_pair(first_block, c))
-            work.append(cross_rows(first_block, c, BLK // 16, BLK // 8))
+            work.append(cross_rows(group, c, 0, BLK // 16))
+            work.append(modal(group, c))
+            work.append(cross_rows(group, c, BLK // 16, BLK // 8))
         return work
 
-    for pair in range(0, blocks, 2):
-        for b in (pair, pair + 1):
+    groups = SCHEDULE
+    work = []
+    for group in groups:
+        products = []
+        for b in group:
             for copy in block_copies[b]:
                 copy.wait()
-        products = transform(pair) + transform(pair + 1)
-        work = pair_work(pair - 2) if pair else []
+            products += transform(b)
+        done = 0
         for k, product in enumerate(products):
+            upto = (k + 1) * len(work) // len(products)
+            for emit in work[done:upto]:
+                emit()
+            done = upto
             product()
-            if k < len(work):
-                work[k]()
-    for emit in pair_work(blocks - 2):
+        work = vector_work(group)
+    for emit in work:
         emit()
     table_copies[2].wait()
     for c in range(tiles):
@@ -236,30 +243,53 @@
             out_ref[:, group * LANES:(group + 1) * LANES] = packed[group]
 
 
-def nearby_kernel(nodes, blocks, gr_ref, rate_ref, res_ref, skip_ref, fwd_ref, inv_ref, lift_ref,
-                  near_ref, weighted_ref, impulse, filt):
+def nearby_kernel(nodes, blocks, gr_hbm, rate_ref, res_ref, skip_ref, fwd_hbm, inv_hbm, lift_hbm,
+                  near_ref, weighted_ref, gr_ref, fwd_ref, inv_ref, lift_ref, impulse, filt, response,
+                  table_sem, gr_sem):
+    channels = rate_ref.shape[1]
+    tiles = channels // TILE
+
+    def table_in(k):
+        src, dst = ((lift_hbm, lift_ref), (fwd_hbm, fwd_ref), (inv_hbm, inv_ref))[k]
+        return pltpu.make_async_copy(src, dst, table_sem.at[k])
+
+    def block_in(b):
+        rows = pl.ds(b * BLK, BLK)
+        return pltpu.make_async_copy(gr_hbm.at[rows, :], gr_ref.at[rows, :], gr_sem.at[b])
+
+    for k in range(3):
+        table_in(k).start()
+    for b in range(blocks):
+        block_in(b).start()
+
     rates = jnp.exp(rate_ref[...])
-    root = jnp.sqrt(rates)
-    residues = res_ref[...]
-    weights = 0.25 * residues * root
+    weights = 0.25 * res_ref[...] * jnp.sqrt(rates)
     for n in range(NODES):
         weighted = weights * jnp.exp(rates * (-nodes[n]))
-        weighted_ref[pl.ds(n * MODES, MODES), :] = weighted
+        weighted_ref[n * MODES:(n + 1) * MODES, :] = weighted
         impulse[n:n + 1, :] = jnp.sum(weighted, axis=0, keepdims=True)
     high, low = halves(impulse[...])
+    table_in(0).wait()
     filt[...] = dot32(lift_ref[...], jnp.concatenate([high, low, high], axis=0))
     skip = skip_ref[...]
-
+    table_in(1).wait()
+    table_in(2).wait()
     for b in range(blocks):
+        block_in(b).wait()
         rows = slice(b * BLK, (b + 1) * BLK)
-        grad = gr_ref[rows, :]
-        spec = dot32(fwd_ref[...], grad)
-        gc, gs = spec[:BLK], spec[BLK:]
-        hc, hs = filt[:BLK, :], filt[BLK:, :]
-        real = (gc * hc + gs * hs).astype(jnp.bfloat16)
-        imag = (gc * hs - gs * hc).astype(jnp.bfloat16)
-        near = dot32(inv_ref[:, :BLK], real) + dot32(inv_ref[:, BLK:], imag)
-        near_ref[rows, :] = near + skip * grad.astype(jnp.float32)
+        slot = b % 2
+        for c in range(tiles):
+            lanes = slice(c * TILE, (c + 1) * TILE)
+            spec = dot32(fwd_ref[...], gr_ref[rows, lanes])
+            gc, gs = spec[:BLK], spec[BLK:]
+            hc, hs = filt[:BLK, lanes], filt[BLK:, lanes]
+            response[slot, :BLK, lanes] = (gc * hc + gs * hs).astype(jnp.bfloat16)
+            response[slot, BLK:, lanes] = (gc * hs - gs * hc).astype(jnp.bfloat16)
+        for c in range(tiles):
+            lanes = slice(c * TILE, (c + 1) * TILE)
+            near = dot32(inv_ref[...], response[slot, :, lanes])
+            near = near + skip[:, lanes] * gr_ref[rows, lanes].astype(jnp.float32)
+            near_ref[rows, lanes] = near.astype(NEAR_TYPE)
 
 
 def scan_kernel(shards, span, in_ref, out_ref):
@@ -284,22 +314,15 @@
         back = row(d, 4) + decay * back
 
 
-def finish_kernel(blocks, scaling, near_hbm, mid_ref, weighted_ref, local_ref, rate_ref, res_ref, spread_ref,
-                  out_hbm, gres_ref, grate_ref, gskip_ref, near_ref, out_ref, packed, back_scr, coef,
-                  near_sem, out_sem):
+def finish_kernel(blocks, scaling, near_ref, mid_ref, weighted_ref, local_ref, rate_ref, res_ref, spread_ref,
+                  out_hbm, gres_hbm, grate_hbm, gskip_hbm, out_ref, gres_ref, grate_ref, gskip_ref,
+                  packed, back_scr, coef, out_sem, grad_sem):
     channels = rate_ref.shape[1]
     groups = channels // LANES
-
-    def near_in(b):
-        rows = pl.ds(b * BLK, BLK)
-        return pltpu.make_async_copy(near_hbm.at[rows, :], near_ref.at[rows, :], near_sem.at[b])
 
     def block_out(b):
         rows = pl.ds(b * BLK, BLK)
         return pltpu.make_async_copy(out_ref.at[rows, :], out_hbm.at[rows, :], out_sem.at[b])
-
-    for b in range(blocks):
-        near_in(b).start()
 
     rates = jnp.exp(rate_ref[...])
     residues = res_ref[...]
@@ -314,6 +337,17 @@
             [packed[lane, pl.ds(q, MODES, stride=ROWS), :] for lane in range(groups)], axis=1
         )
 
+    first, second = picked(1), picked(2)
+    gres_ref[...] = 0.25 * root * first * scaling
+    grate_ref[...] = (0.125 * residues * root * first - rates * weights * second) * scaling
+    gskip_ref[...] = mid_ref[3:4, :] * scaling
+    grad_copies = [
+        pltpu.make_async_copy(src, dst, grad_sem.at[k])
+        for k, (src, dst) in enumerate(((gres_ref, gres_hbm), (grate_ref, grate_hbm), (gskip_ref, gskip_hbm)))
+    ]
+    for copy in grad_copies:
+        copy.start()
+
     back = picked(0)
     for b in reversed(range(blocks)):
         for lane in range(groups):
@@ -321,11 +355,11 @@
         back = local_ref[b * MODES:(b + 1) * MODES, :] + step_decay * back
     for lane in range(groups):
         span = slice(lane * LANES, (lane + 1) * LANES)
+        backs = [back_scr[lane, m * blocks:(m + 1) * blocks, :] for m in range(MODES)]
         for n in range(NODES):
             total = jnp.zeros((blocks, LANES), jnp.float32)
             for m in range(MODES):
-                line = weighted_ref[n * MODES + m:n * MODES + m + 1, span]
-                total = total + back_scr[lane, m * blocks:(m + 1) * blocks, :] * line
+                total = total + backs[m] * weighted_ref[n * MODES + m:n * MODES + m + 1, span]
             coef[lane, pl.ds(n, blocks, stride=NODES), :] = total
     for b in range(blocks):
         high, low = halves(
@@ -333,15 +367,12 @@
         )
         far = dot32(spread_ref[...], jnp.concatenate([high, low, high], axis=0))
         rows = slice(b * BLK, (b + 1) * BLK)
-        near_in(b).wait()
         out_ref[rows, :] = (near_ref[rows, :] + far).astype(jnp.bfloat16)
         block_out(b).start()
-    first, second = picked(1), picked(2)
-    gres_ref[...] = 0.25 * root * first * scaling
-    grate_ref[...] = (0.125 * residues * root * first - rates * weights * second) * scaling
-    gskip_ref[...] = mid_ref[3:4, :] * scaling
     for b in range(blocks):
         block_out(b).wait()
+    for copy in grad_copies:
+        copy.wait()
 
 
 def cols(rows):
@@ -361,6 +392,10 @@
 
 
 PARAMS = pltpu.CompilerParams(vmem_limit_bytes=VMEM_LIMIT)
+
+
+def in_hbm(array):
+    return pltpu.with_memory_space_constraint(array, pltpu.HBM)
 
 
 def call_sums(inputs, grad_out, log_rates):
@@ -395,23 +430,35 @@
         ],
         compiler_params=PARAMS,
         cost_estimate=cost(4 * spec_rows * tokens * channels, 8 * tokens * channels),
-    )(*(pltpu.with_memory_space_constraint(x, pltpu.HBM) for x in (inputs, grad_out, log_rates, *consts)))
+    )(*map(in_hbm, (inputs, grad_out, log_rates, *consts)))
 
 
 def call_nearby(grad_out, log_rates, residues, skip_line):
     tokens, channels = grad_out.shape
     t = tables()
     consts = [jnp.asarray(t[k]) for k in ("forward", "inverse", "lift")]
+    blocks = tokens // BLK
+    far = pl.BlockSpec(memory_space=pltpu.HBM)
+    near = pl.BlockSpec(memory_space=pltpu.VMEM)
     return pl.pallas_call(
-        functools.partial(nearby_kernel, t["nodes"], tokens // BLK),
-        grid=(channels // TILE,),
-        in_specs=[cols(tokens), cols(MODES), cols(MODES), cols(1)] + [whole(c) for c in consts],
-        out_specs=[cols(tokens), cols(NODES * MODES)],
-        out_shape=[f32_rows(tokens, channels), f32_rows(NODES * MODES, channels)],
-        scratch_shapes=[pltpu.VMEM((NODES, TILE), jnp.float32), pltpu.VMEM((2 * BLK, TILE), jnp.float32)],
+        functools.partial(nearby_kernel, t["nodes"], blocks),
+        in_specs=[far, near, near, near, far, far, far],
+        out_specs=[near, near],
+        out_shape=[jax.ShapeDtypeStruct((tokens, channels), NEAR_TYPE), f32_rows(NODES * MODES, channels)],
+        scratch_shapes=[
+            pltpu.VMEM((tokens, channels), jnp.bfloat16),
+            pltpu.VMEM(consts[0].shape, jnp.bfloat16),
+            pltpu.VMEM(consts[1].shape, jnp.bfloat16),
+            pltpu.VMEM(consts[2].shape, jnp.bfloat16),
+            pltpu.VMEM((NODES, channels), jnp.float32),
+            pltpu.VMEM((2 * BLK, channels), jnp.float32),
+            pltpu.VMEM((2, 2 * BLK, channels), jnp.bfloat16),
+            pltpu.SemaphoreType.DMA((3,)),
+            pltpu.SemaphoreType.DMA((blocks,)),
+        ],
         compiler_params=PARAMS,
         cost_estimate=cost(8 * BLK * tokens * channels, 6 * tokens * channels),
-    )(grad_out, log_rates, residues, skip_line, *consts)
+    )(in_hbm(grad_out), log_rates, residues, skip_line, *map(in_hbm, consts))
 
 
 def call_scan(by_mode, tokens):
@@ -430,8 +477,8 @@
     near = pl.BlockSpec(memory_space=pltpu.VMEM)
     return pl.pallas_call(
         functools.partial(finish_kernel, blocks, scaling),
-        in_specs=[far] + [near] * 6,
-        out_specs=[far, near, near, near],
+        in_specs=[near] * 7,
+        out_specs=[far] * 4,
         out_shape=[
             jax.ShapeDtypeStruct((tokens, channels), jnp.bfloat16),
             f32_rows(MODES, channels),
@@ -439,16 +486,18 @@
             f32_rows(1, channels),
         ],
         scratch_shapes=[
-            pltpu.VMEM((tokens, channels), nearby.dtype),
             pltpu.VMEM((tokens, channels), jnp.bfloat16),
+            pltpu.VMEM((MODES, channels), jnp.float32),
+            pltpu.VMEM((MODES, channels), jnp.float32),
+            pltpu.VMEM((1, channels), jnp.float32),
             pltpu.VMEM((channels // LANES, MODES * ROWS, LANES), jnp.float32),
             pltpu.VMEM((channels // LANES, MODES * blocks, LANES), jnp.float32),
             pltpu.VMEM((channels // LANES, NODES * blocks, LANES), jnp.float32),
             pltpu.SemaphoreType.DMA((blocks,)),
-            pltpu.SemaphoreType.DMA((blocks,)),
+            pltpu.SemaphoreType.DMA((3,)),
         ],
         compiler_params=PARAMS,
-    )(pltpu.with_memory_space_constraint(nearby, pltpu.HBM), back, weighted, local, log_rates, residues, spread)
+    )(nearby, back, weighted, local, log_rates, residues, spread)
 
 
 def on_device(inputs, grad_out, residues, log_rates, skip_weight):

time: 42.2 us -> 39.1 us (0.927)
  local copies, waits for them, and re-layouts: 4.76 us -> 0.02 us
  waiting for transfers between devices: 0.01 us -> 1.68 us
    unnamed x18 -> x8, local copies, waits for them, and re-layouts: 4.76 us -> 0.02 us
    pallas_call x1, Pallas kernels: 4.26 us -> 6.74 us  [call_nearby(): pl.pallas_call(functools.partial(nearby_kernel, t['nodes'], blocks), in_s...]
    pallas_call x1, Pallas kernels: 4.15 us -> 2.16 us  [call_finish(): pl.pallas_call(functools.partial(finish_kernel, blocks, scaling), in_spec...]
    all_to_all x1, waiting for transfers between devices: 0.01 us -> 1.68 us  [on_device(): lax.all_to_all(scanned, 'ctx', split_axis=0, concat_axis=0, tiled=True)]
  transfers between devices with their start and end apart: 1 -> 1, of which waited for: 0 -> 1; matrix products, arithmetic and copies ran while one was open for 0% -> 0% of each run, Pallas kernels for 10% -> 17%
where the time goes in v2:
time: 39.1 us; the launch traced here: 38.8 us
  Pallas kernels  17.4 us (45%)
  blocking collectives  15.4 us (39%)
  starting transfers between devices  3.63 us (9%)
  waiting for transfers between devices  1.68 us (4%)
  between operations  0.71 us (2%)
    all_to_all x1, blocking collectives, on_device(): lax.all_to_all(summed.reshape(MODES, ROWS, channels), 'ctx', split_axis=0...  15.4 us
    pallas_call x1, Pallas kernels, call_sums(): pl.pallas_call(functools.partial(sums_kernel, t['nodes'], blocks), in_spe...  7.66 us
    pallas_call x1, Pallas kernels, call_nearby(): pl.pallas_call(functools.partial(nearby_kernel, t['nodes'], blocks), in_s...  6.74 us
    all_to_all x1, starting transfers between devices, on_device(): lax.all_to_all(scanned, 'ctx', split_axis=0, concat_axis=0, tiled=True)  3.63 us
    pallas_call x1, Pallas kernels, call_finish(): pl.pallas_call(functools.partial(finish_kernel, blocks, scaling), in_spec...  2.16 us
    all_to_all x1, waiting for transfers between devices, on_device(): lax.all_to_all(scanned, 'ctx', split_axis=0, concat_axis=0, tiled=True)  1.68 us
    pallas_call x1, Pallas kernels, call_scan(): pl.pallas_call(functools.partial(scan_kernel, by_mode.shape[0], float(tok...  0.8 us
  transfers between devices with their start and end apart: 1, of which 1 were waited for; matrix products, arithmetic and copies ran while one was open for 0% of the time, Pallas kernels for 17%

profile of v2, /device:TPU:0, one launch (start us, length us, event | category | flops | bytes accessed | tf_op | source)
XLA Modules:
  0.0 38.8 jit_solution(7186137715309895141)
XLA Ops:
  0.6 0.0 copy-start.1
  0.6 0.0 copy-start.2
  0.7 0.0 copy-start.3
  0.7 7.7 %shard_map.148 = (f32[128,512]{1,0:T(8,128)S(1)}, f32[128,512]{1,0:T(8,128)S(1)}) custom-call(bf16[2048,512]{1,0:T(8,128)(2,1)} %in_hbm.1, bf16[2048,512]{1,0:T(8,128)(2,1)} %gr_hbm.3, f32[16,512]{1,0:T(8,128)} %bitcast.10, bf16[560,256]{1,0:T(8,128)(2,1)} %constant.14.clone.tin_hbm, bf16[560,256]{1,0:T(8,128)(2,1)} %constant.15.clone.tgr_hbm, ...), custom_call_target="tpu_custom_call" | custom-call | flops 2348810240 | bytes 8388608 | tf_op jit(solution)/shard_map/pallas_call | solution.py:409
  8.3 15.4 %all_to_all.10.in_ref = f32[16,8,512]{2,1,0:T(8,128)S(1)} all-to-all(f32[16,8,512]{2,1,0:T(8,128)S(1)} %bitcast.9), channel_id=1, replica_groups=mesh['ctx'=16,'ch'=8] {'ctx'}, dimensions={0} | all-to-all | bytes 524288 | tf_op jit(solution)/shard_map/all_to_all | solution.py:508
  23.8 0.8 %shard_map.149 = f32[16,8,512]{2,1,0:T(8,128)} custom-call(f32[16,8,512]{2,1,0:T(8,128)S(1)} %all_to_all.10.in_ref), custom_call_target="tpu_custom_call" | custom-call | tf_op jit(solution)/shard_map/pallas_call | solution.py:465
  24.6 3.6 %all-to-all-start.1 = ((f32[16,8,512]{2,1,0:T(8,128)}), f32[16,8,512]{2,1,0:T(8,128)S(1)}, u32[]{:S(2)}, u32[]{:S(2)}) async-start(f32[16,8,512]{2,1,0:T(8,128)} %shard_map.149), calls=%async_computation.1 | async-start | bytes 524288 | tf_op jit(solution)/shard_map/all_to_all | solution.py:513
  28.2 0.0 copy-done.1
  28.2 0.0 copy-done.2
  28.2 0.0 copy-done.3
  28.2 0.0 copy-start
  28.2 6.7 %shard_map.147 = (bf16[2048,512]{1,0:T(8,128)(2,1)S(1)}, f32[384,512]{1,0:T(8,128)S(1)}) custom-call(bf16[2048,512]{1,0:T(8,128)(2,1)} %gr_hbm.3, f32[16,512]{1,0:T(8,128)S(1)} %bitcast.11, f32[16,512]{1,0:T(8,128)S(1)} %bitcast.13, f32[1,512]{1,0:T(1,128)S(1)} %bitcast.15, bf16[512,256]{1,0:T(8,128)(2,1)} %constant.17.clone.fwd_hbm, ...), custom_call_target="tpu_custom_call" | custom-call | flops 2147483648 | bytes 6291456 | tf_op jit(solution)/shard_map/pallas_call | solution.py:443
  35.0 1.7 %all-to-all-done.1 = f32[16,8,512]{2,1,0:T(8,128)S(1)} async-done(((f32[16,8,512]{2,1,0:T(8,128)}), f32[16,8,512]{2,1,0:T(8,128)S(1)}, u32[]{:S(2)}, u32[]{:S(2)}) %all-to-all-start.1) | async-done | bytes 262176 | tf_op jit(solution)/shard_map/all_to_all | solution.py:513
  36.7 0.0 copy-done
  36.7 2.2 %shard_map.150 = (bf16[2048,512]{1,0:T(8,128)(2,1)}, f32[16,512]{1,0:T(8,128)}, f32[16,512]{1,0:T(8,128)}, f32[1,512]{1,0:T(1,128)}) custom-call(bf16[2048,512]{1,0:T(8,128)(2,1)S(1)} %get-tuple-element.12.near_ref, f32[128,512]{1,0:T(8,128)S(1)} %bitcast.8, f32[384,512]{1,0:T(8,128)S(1)} %get-tuple-element.14.weighted_ref, ...), custom_call_target="tpu_custom_call" | custom-call | tf_op jit(solution)/shard_map/pallas_call | solution.py:478
Async XLA Ops:
  0.6 27.6 %copy-start.1 = (f32[512,16]{0,1:T(8,128)S(1)}, f32[512,16]{0,1:T(8,128)}, u32[]{:S(2)}) copy-start(f32[512,16]{0,1:T(8,128)} %param.15) | copy-start | bytes 98308
  0.6 27.6 %copy-start.2 = (f32[512,16]{0,1:T(8,128)S(1)}, f32[512,16]{0,1:T(8,128)}, u32[]{:S(2)}) copy-start(f32[512,16]{0,1:T(8,128)} %param.14) | copy-start | bytes 98308
  0.7 27.6 %copy-start.3 = (f32[512]{0:T(512)S(1)}, f32[512]{0:T(512)}, u32[]{:S(2)}) copy-start(f32[512]{0:T(512)} %param.16) | copy-start | bytes 6148
  24.6 12.1 %all-to-all-start.1 = ((f32[16,8,512]{2,1,0:T(8,128)}), f32[16,8,512]{2,1,0:T(8,128)S(1)}, u32[]{:S(2)}, u32[]{:S(2)}) async-start(f32[16,8,512]{2,1,0:T(8,128)} %shard_map.149), calls=%async_computation.1 | async-start | bytes 524288 | tf_op jit(solution)/shard_map/all_to_all | solution.py:513
  28.2 8.4 %copy-start = (bf16[256,72]{1,0:T(8,128)(2,1)S(1)}, bf16[256,72]{1,0:T(8,128)(2,1)}, u32[]{:S(2)}) copy-start(bf16[256,72]{1,0:T(8,128)(2,1)} %constant.20.clone.spread_ref) | copy-start | bytes 110596

commit v3 on v2

--- a/solution.py
+++ b/solution.py
@@ -307,10 +307,15 @@
         skip = skip + row(d, 6)
         mom_in = decay * (mom_in + span * sum_in) + row(d, 3)
         sum_in = decay * sum_in + row(d, 2)
-    blank = jnp.zeros((4, first.shape[1]), jnp.float32)
+    width = first.shape[1] // 2
+
+    def folded(line):
+        return [line[:, :width], line[:, width:]]
+
+    sums = folded(first) + folded(second) + folded(skip)
     back = zero
     for d in reversed(range(shards)):
-        out_ref[d] = jnp.concatenate([back, first, second, skip, blank], axis=0)
+        out_ref[d] = jnp.concatenate(folded(back) + sums, axis=0)
         back = row(d, 4) + decay * back
 
 
@@ -329,18 +334,23 @@
     root = jnp.sqrt(rates)
     weights = 0.25 * residues * root
     step_decay = jnp.exp(rates * (-float(BLK)))
-    for lane in range(groups):
+    folds = groups // 2
+    for lane in range(folds):
         packed[lane] = mid_ref[:, lane * LANES:(lane + 1) * LANES]
 
     def picked(q):
         return jnp.concatenate(
-            [packed[lane, pl.ds(q, MODES, stride=ROWS), :] for lane in range(groups)], axis=1
+            [
+                packed[lane % folds, pl.ds(2 * q + lane // folds, MODES, stride=ROWS), :]
+                for lane in range(groups)
+            ],
+            axis=1,
         )
 
     first, second = picked(1), picked(2)
     gres_ref[...] = 0.25 * root * first * scaling
     grate_ref[...] = (0.125 * residues * root * first - rates * weights * second) * scaling
-    gskip_ref[...] = mid_ref[3:4, :] * scaling
+    gskip_ref[...] = jnp.concatenate([mid_ref[6:7, :], mid_ref[7:8, :]], axis=1) * scaling
     grad_copies = [
         pltpu.make_async_copy(src, dst, grad_sem.at[k])
         for k, (src, dst) in enumerate(((gres_ref, gres_hbm), (grate_ref, grate_hbm), (gskip_ref, gskip_hbm)))
@@ -462,9 +472,10 @@
 
 
 def call_scan(by_mode, tokens):
+    shards, rows, channels = by_mode.shape
     return pl.pallas_call(
-        functools.partial(scan_kernel, by_mode.shape[0], float(tokens)),
-        out_shape=jax.ShapeDtypeStruct(by_mode.shape, jnp.float32),
+        functools.partial(scan_kernel, shards, float(tokens)),
+        out_shape=jax.ShapeDtypeStruct((shards, rows, channels // 2), jnp.float32),
         compiler_params=PARAMS,
     )(by_mode)
 
@@ -490,7 +501,7 @@
             pltpu.VMEM((MODES, channels), jnp.float32),
             pltpu.VMEM((MODES, channels), jnp.float32),
             pltpu.VMEM((1, channels), jnp.float32),
-            pltpu.VMEM((channels // LANES, MODES * ROWS, LANES), jnp.float32),
+            pltpu.VMEM((channels // LANES // 2, MODES * ROWS, LANES), jnp.float32),
             pltpu.VMEM((channels // LANES, MODES * blocks, LANES), jnp.float32),
             pltpu.VMEM((channels // LANES, NODES * blocks, LANES), jnp.float32),
             pltpu.SemaphoreType.DMA((blocks,)),
@@ -512,7 +523,7 @@
     scanned = call_scan(by_mode, tokens)
     back = lax.all_to_all(scanned, "ctx", split_axis=0, concat_axis=0, tiled=True)
     grad_inputs, grad_residues, grad_log_rates, grad_skip = call_finish(
-        scaling, nearby, back.reshape(MODES * ROWS, channels), weighted, local, log_rates, residues
+        scaling, nearby, back.reshape(MODES * ROWS, channels // 2), weighted, local, log_rates, residues
     )
     return grad_inputs, grad_residues.T, grad_log_rates.T, grad_skip.reshape(channels)
 

time: 39.1 us -> 38.4 us (0.982)
  waiting for transfers between devices: 1.68 us -> 1.05 us
    all_to_all x1, waiting for transfers between devices: 1.68 us -> 1.05 us  [on_device(): lax.all_to_all(scanned, 'ctx', split_axis=0, concat_axis=0, tiled=True)]
  transfers between devices with their start and end apart: 1 -> 1, of which waited for: 1 -> 1; matrix products, arithmetic and copies ran while one was open for 0% -> 0% of each run, Pallas kernels for 17% -> 18%
where the time goes in v3:
time: 38.4 us; the launch traced here: 38.2 us
  Pallas kernels  17.3 us (45%)
  blocking collectives  15.4 us (40%)
  starting transfers between devices  3.63 us (9%)
  waiting for transfers between devices  1.05 us (3%)
  between operations  0.71 us (2%)
    all_to_all x1, blocking collectives, on_device(): lax.all_to_all(summed.reshape(MODES, ROWS, channels), 'ctx', split_axis=0...  15.4 us
    pallas_call x1, Pallas kernels, call_sums(): pl.pallas_call(functools.partial(sums_kernel, t['nodes'], blocks), in_spe...  7.66 us
    pallas_call x1, Pallas kernels, call_nearby(): pl.pallas_call(functools.partial(nearby_kernel, t['nodes'], blocks), in_s...  6.74 us
    all_to_all x1, starting transfers between devices, on_device(): lax.all_to_all(scanned, 'ctx', split_axis=0, concat_axis=0, tiled=True)  3.63 us
    pallas_call x1, Pallas kernels, call_finish(): pl.pallas_call(functools.partial(finish_kernel, blocks, scaling), in_spec...  2.16 us
    all_to_all x1, waiting for transfers between devices, on_device(): lax.all_to_all(scanned, 'ctx', split_axis=0, concat_axis=0, tiled=True)  1.05 us
  transfers between devices with their start and end apart: 1, of which 1 were waited for; matrix products, arithmetic and copies ran while one was open for 0% of the time, Pallas kernels for 18%

profile of v3, /device:TPU:0, one launch (start us, length us, event | category | flops | bytes accessed | tf_op | source)
XLA Modules:
  0.0 38.2 jit_solution(5032980281642414712)
XLA Ops:
  0.6 0.0 copy-start.1
  0.6 0.0 copy-start.2
  0.7 0.0 copy-start.3
  0.7 7.7 %shard_map.148 = (f32[128,512]{1,0:T(8,128)S(1)}, f32[128,512]{1,0:T(8,128)S(1)}) custom-call(bf16[2048,512]{1,0:T(8,128)(2,1)} %in_hbm.1, bf16[2048,512]{1,0:T(8,128)(2,1)} %gr_hbm.3, f32[16,512]{1,0:T(8,128)} %bitcast.10, bf16[560,256]{1,0:T(8,128)(2,1)} %constant.14.clone.tin_hbm, bf16[560,256]{1,0:T(8,128)(2,1)} %constant.15.clone.tgr_hbm, ...), custom_call_target="tpu_custom_call" | custom-call | flops 2348810240 | bytes 8388608 | tf_op jit(solution)/shard_map/pallas_call | solution.py:419
  8.3 15.4 %all_to_all.10.in_ref = f32[16,8,512]{2,1,0:T(8,128)S(1)} all-to-all(f32[16,8,512]{2,1,0:T(8,128)S(1)} %bitcast.9), channel_id=1, replica_groups=mesh['ctx'=16,'ch'=8] {'ctx'}, dimensions={0} | all-to-all | bytes 524288 | tf_op jit(solution)/shard_map/all_to_all | solution.py:519
  23.8 0.8 %shard_map.149 = f32[16,8,256]{2,1,0:T(8,128)} custom-call(f32[16,8,512]{2,1,0:T(8,128)S(1)} %all_to_all.10.in_ref), custom_call_target="tpu_custom_call" | custom-call | tf_op jit(solution)/shard_map/pallas_call | solution.py:476
  24.5 3.6 %all-to-all-start.1 = ((f32[16,8,256]{2,1,0:T(8,128)}), f32[16,8,256]{2,1,0:T(8,128)S(1)}, u32[]{:S(2)}, u32[]{:S(2)}) async-start(f32[16,8,256]{2,1,0:T(8,128)} %shard_map.149), calls=%async_computation.1 | async-start | bytes 262144 | tf_op jit(solution)/shard_map/all_to_all | solution.py:524
  28.1 0.0 copy-done.1
  28.2 0.0 copy-done.2
  28.2 0.0 copy-done.3
  28.2 0.0 copy-start
  28.2 6.7 %shard_map.147 = (bf16[2048,512]{1,0:T(8,128)(2,1)S(1)}, f32[384,512]{1,0:T(8,128)S(1)}) custom-call(bf16[2048,512]{1,0:T(8,128)(2,1)} %gr_hbm.3, f32[16,512]{1,0:T(8,128)S(1)} %bitcast.11, f32[16,512]{1,0:T(8,128)S(1)} %bitcast.13, f32[1,512]{1,0:T(1,128)S(1)} %bitcast.15, bf16[512,256]{1,0:T(8,128)(2,1)} %constant.17.clone.fwd_hbm, ...), custom_call_target="tpu_custom_call" | custom-call | flops 2147483648 | bytes 6291456 | tf_op jit(solution)/shard_map/pallas_call | solution.py:453
  34.9 1.0 %all-to-all-done.1 = f32[16,8,256]{2,1,0:T(8,128)S(1)} async-done(((f32[16,8,256]{2,1,0:T(8,128)}), f32[16,8,256]{2,1,0:T(8,128)S(1)}, u32[]{:S(2)}, u32[]{:S(2)}) %all-to-all-start.1) | async-done | bytes 131104 | tf_op jit(solution)/shard_map/all_to_all | solution.py:524
  36.0 0.0 copy-done
  36.0 2.2 %shard_map.150 = (bf16[2048,512]{1,0:T(8,128)(2,1)}, f32[16,512]{1,0:T(8,128)}, f32[16,512]{1,0:T(8,128)}, f32[1,512]{1,0:T(1,128)}) custom-call(bf16[2048,512]{1,0:T(8,128)(2,1)S(1)} %get-tuple-element.12.near_ref, f32[128,256]{1,0:T(8,128)S(1)} %bitcast.8, f32[384,512]{1,0:T(8,128)S(1)} %get-tuple-element.14.weighted_ref, ...), custom_call_target="tpu_custom_call" | custom-call | tf_op jit(solution)/shard_map/pallas_call | solution.py:489
Async XLA Ops:
  0.6 27.5 %copy-start.1 = (f32[512,16]{0,1:T(8,128)S(1)}, f32[512,16]{0,1:T(8,128)}, u32[]{:S(2)}) copy-start(f32[512,16]{0,1:T(8,128)} %param.15) | copy-start | bytes 98308
  0.6 27.5 %copy-start.2 = (f32[512,16]{0,1:T(8,128)S(1)}, f32[512,16]{0,1:T(8,128)}, u32[]{:S(2)}) copy-start(f32[512,16]{0,1:T(8,128)} %param.14) | copy-start | bytes 98308
  0.7 27.5 %copy-start.3 = (f32[512]{0:T(512)S(1)}, f32[512]{0:T(512)}, u32[]{:S(2)}) copy-start(f32[512]{0:T(512)} %param.16) | copy-start | bytes 6148
  24.5 11.5 %all-to-all-start.1 = ((f32[16,8,256]{2,1,0:T(8,128)}), f32[16,8,256]{2,1,0:T(8,128)S(1)}, u32[]{:S(2)}, u32[]{:S(2)}) async-start(f32[16,8,256]{2,1,0:T(8,128)} %shard_map.149), calls=%async_computation.1 | async-start | bytes 262144 | tf_op jit(solution)/shard_map/all_to_all | solution.py:524
  28.2 7.8 %copy-start = (bf16[256,72]{1,0:T(8,128)(2,1)S(1)}, bf16[256,72]{1,0:T(8,128)(2,1)}, u32[]{:S(2)}) copy-start(bf16[256,72]{1,0:T(8,128)(2,1)} %constant.20.clone.spread_ref) | copy-start | bytes 110596

commit v4 on v3

--- a/solution.py
+++ b/solution.py
@@ -234,13 +234,13 @@
         totals, moments = contract(c, [folded[:NODES]])
         first, second, sum_in, mom_in, gsum, gmom, _ = state[c]
         skip_rows = jnp.broadcast_to(folded[NODES:NODES + 1], (MODES, TILE))
-        parts = (first + totals[0], second + moments[0], sum_in, mom_in, gsum, gmom, skip_rows, rates[:, lanes(c)])
+        parts = (first + totals[0], second + moments[0], sum_in, mom_in, gsum, gmom, skip_rows, zero)
         for half in range(GROUPS):
             span = slice(half * LANES, (half + 1) * LANES)
-            group = c * GROUPS + half
             for q, part in enumerate(parts):
-                packed[group, pl.ds(q, MODES, stride=ROWS), :] = part[:, span]
-            out_ref[:, group * LANES:(group + 1) * LANES] = packed[group]
+                packed[half, pl.ds(2 * q + c, MODES, stride=2 * ROWS), :] = part[:, span]
+    for half in range(GROUPS):
+        out_ref[:, half * LANES:(half + 1) * LANES] = packed[half].astype(jnp.bfloat16)
 
 
 def nearby_kernel(nodes, blocks, gr_hbm, rate_ref, res_ref, skip_ref, fwd_hbm, inv_hbm, lift_hbm,
@@ -292,31 +292,27 @@
             near_ref[rows, lanes] = near.astype(NEAR_TYPE)
 
 
-def scan_kernel(shards, span, in_ref, out_ref):
-    decay = jnp.exp(in_ref[0, 7:8, :] * (-span))
-
-    def row(d, q):
-        return in_ref[d, q:q + 1, :]
-
+def scan_kernel(shards, span, in_ref, rate_ref, out_ref):
+    line = rate_ref[pl.ds(lax.axis_index("ctx"), 1), :]
+    width = line.shape[1] // 2
+    rates = jnp.exp(jnp.concatenate([line[:, :width], line[:, width:]], axis=0))
+    decay = jnp.exp(rates * (-span))
     zero = jnp.zeros_like(decay)
     first, second, skip, sum_in, mom_in = zero, zero, zero, zero, zero
+    gsums = []
     for d in range(shards):
-        gsum, gmom = row(d, 4), row(d, 5)
-        first = first + (row(d, 0) + gsum * sum_in)
-        second = second + (row(d, 1) + (gmom * sum_in + gsum * mom_in))
-        skip = skip + row(d, 6)
-        mom_in = decay * (mom_in + span * sum_in) + row(d, 3)
-        sum_in = decay * sum_in + row(d, 2)
-    width = first.shape[1] // 2
-
-    def folded(line):
-        return [line[:, :width], line[:, width:]]
-
-    sums = folded(first) + folded(second) + folded(skip)
+        rows = in_ref[d].astype(jnp.float32)
+        f_part, s_part, u_sum, u_mom, gsum, gmom, k_part = [rows[2 * q:2 * q + 2] for q in range(7)]
+        first = first + (f_part + gsum * sum_in)
+        second = second + (s_part + (gmom * sum_in + gsum * mom_in))
+        skip = skip + k_part
+        mom_in = decay * (mom_in + span * sum_in) + u_mom
+        sum_in = decay * sum_in + u_sum
+        gsums.append(gsum)
     back = zero
     for d in reversed(range(shards)):
-        out_ref[d] = jnp.concatenate(folded(back) + sums, axis=0)
-        back = row(d, 4) + decay * back
+        out_ref[d] = jnp.concatenate([back, first, second, skip], axis=0)
+        back = gsums[d] + decay * back
 
 
 def finish_kernel(blocks, scaling, near_ref, mid_ref, weighted_ref, local_ref, rate_ref, res_ref, spread_ref,
@@ -420,7 +416,10 @@
         functools.partial(sums_kernel, t["nodes"], blocks),
         in_specs=[far] * 6,
         out_specs=[near, near],
-        out_shape=[f32_rows(MODES * ROWS, channels), f32_rows(MODES * blocks, channels)],
+        out_shape=[
+            jax.ShapeDtypeStruct((2 * MODES * ROWS, channels // 2), jnp.bfloat16),
+            f32_rows(MODES * blocks, channels),
+        ],
         scratch_shapes=[
             pltpu.VMEM((MODES, channels), jnp.float32),
             pltpu.VMEM((tokens, channels), jnp.bfloat16),
@@ -433,7 +432,7 @@
             pltpu.VMEM((NODES * MODES, channels), jnp.float32),
             pltpu.VMEM((channels // TILE, 4, NODES, TILE), jnp.float32),
             pltpu.VMEM((2 * BLK, channels), jnp.float32),
-            pltpu.VMEM((channels // LANES, MODES * ROWS, LANES), jnp.float32),
+            pltpu.VMEM((GROUPS, 2 * MODES * ROWS, LANES), jnp.float32),
             pltpu.SemaphoreType.DMA((4,)),
             pltpu.SemaphoreType.DMA((blocks,)),
             pltpu.SemaphoreType.DMA((blocks,)),
@@ -471,13 +470,13 @@
     )(in_hbm(grad_out), log_rates, residues, skip_line, *map(in_hbm, consts))
 
 
-def call_scan(by_mode, tokens):
-    shards, rows, channels = by_mode.shape
+def call_scan(by_mode, tokens, log_rates):
+    shards, _, width = by_mode.shape
     return pl.pallas_call(
         functools.partial(scan_kernel, shards, float(tokens)),
-        out_shape=jax.ShapeDtypeStruct((shards, rows, channels // 2), jnp.float32),
+        out_shape=jax.ShapeDtypeStruct((shards, ROWS, width), jnp.float32),
         compiler_params=PARAMS,
-    )(by_mode)
+    )(by_mode, log_rates)
 
 
 def call_finish(scaling, nearby, back, weighted, local, log_rates, residues):
@@ -517,10 +516,10 @@
     residues, log_rates = residues.T, log_rates.T
     summed, local = call_sums(inputs, grad_out, log_rates)
     by_mode = lax.all_to_all(
-        summed.reshape(MODES, ROWS, channels), "ctx", split_axis=0, concat_axis=0, tiled=True
+        summed.reshape(MODES, 2 * ROWS, channels // 2), "ctx", split_axis=0, concat_axis=0, tiled=True
     )
     nearby, weighted = call_nearby(grad_out, log_rates, residues, skip_weight.reshape(1, channels))
-    scanned = call_scan(by_mode, tokens)
+    scanned = call_scan(by_mode, tokens, log_rates)
     back = lax.all_to_all(scanned, "ctx", split_axis=0, concat_axis=0, tiled=True)
     grad_inputs, grad_residues, grad_log_rates, grad_skip = call_finish(
         scaling, nearby, back.reshape(MODES * ROWS, channels // 2), weighted, local, log_rates, residues

time: 38.4 us -> 37.8 us (0.984)
  blocking collectives: 15.4 us -> 14.8 us
    all_to_all x1, blocking collectives: 15.4 us -> 14.8 us  [on_device(): lax.all_to_all(summed.reshape(MODES, 2 * ROWS, channels // 2), 'ctx', spl...]
where the time goes in v4:
time: 37.8 us; the launch traced here: 37.5 us
  Pallas kernels  17.4 us (46%)
  blocking collectives  14.8 us (39%)
  starting transfers between devices  3.6 us (10%)
  waiting for transfers between devices  1.06 us (3%)
  between operations  0.71 us (2%)
    all_to_all x1, blocking collectives, on_device(): lax.all_to_all(summed.reshape(MODES, 2 * ROWS, channels // 2), 'ctx', spl...  14.8 us
    pallas_call x1, Pallas kernels, call_sums(): pl.pallas_call(functools.partial(sums_kernel, t['nodes'], blocks), in_spe...  7.7 us
    pallas_call x1, Pallas kernels, call_nearby(): pl.pallas_call(functools.partial(nearby_kernel, t['nodes'], blocks), in_s...  6.74 us
    all_to_all x1, starting transfers between devices, on_device(): lax.all_to_all(scanned, 'ctx', split_axis=0, concat_axis=0, tiled=True)  3.6 us
    pallas_call x1, Pallas kernels, call_finish(): pl.pallas_call(functools.partial(finish_kernel, blocks, scaling), in_spec...  2.17 us
    all_to_all x1, waiting for transfers between devices, on_device(): lax.all_to_all(scanned, 'ctx', split_axis=0, concat_axis=0, tiled=True)  1.06 us
    pallas_call x1, Pallas kernels, call_scan(): pl.pallas_call(functools.partial(scan_kernel, shards, float(tokens)), out...  0.78 us
  transfers between devices with their start and end apart: 1, of which 1 were waited for; matrix products, arithmetic and copies ran while one was open for 0% of the time, Pallas kernels for 18%

profile of v4, /device:TPU:0, one launch (start us, length us, event | category | flops | bytes accessed | tf_op | source)
XLA Modules:
  0.0 37.5 jit_solution(12278961207536551080)
XLA Ops:
  0.6 0.0 copy-start
  0.6 0.0 copy-start.2
  0.7 0.0 copy-start.3
  0.7 7.7 %shard_map.148 = (bf16[256,256]{1,0:T(8,128)(2,1)S(1)}, f32[128,512]{1,0:T(8,128)S(1)}) custom-call(bf16[2048,512]{1,0:T(8,128)(2,1)} %in_hbm.1, bf16[2048,512]{1,0:T(8,128)(2,1)} %gr_hbm.3, f32[16,512]{1,0:T(8,128)} %bitcast.10, bf16[560,256]{1,0:T(8,128)(2,1)} %constant.14.clone.tin_hbm, bf16[560,256]{1,0:T(8,128)(2,1)} %constant.15.clone.tgr_hbm, ...), custom_call_target="tpu_custom_call" | custom-call | flops 2348810240 | bytes 8388608 | tf_op jit(solution)/shard_map/pallas_call | solution.py:415
  8.4 14.8 %all_to_all.10.in_ref = bf16[16,16,256]{2,1,0:T(8,128)(2,1)S(1)} all-to-all(bf16[16,16,256]{2,1,0:T(8,128)(2,1)S(1)} %bitcast.9), channel_id=1, replica_groups=mesh['ctx'=16,'ch'=8] {'ctx'}, dimensions={0} | all-to-all | bytes 262144 | tf_op jit(solution)/shard_map/all_to_all | solution.py:518
  23.1 0.0 copy-done
  23.1 0.8 %shard_map.149 = f32[16,8,256]{2,1,0:T(8,128)} custom-call(bf16[16,16,256]{2,1,0:T(8,128)(2,1)S(1)} %all_to_all.10.in_ref, f32[16,512]{1,0:T(8,128)S(1)} %bitcast.11), custom_call_target="tpu_custom_call" | custom-call | tf_op jit(solution)/shard_map/pallas_call | solution.py:475
  23.9 3.6 %all-to-all-start.1 = ((f32[16,8,256]{2,1,0:T(8,128)}), f32[16,8,256]{2,1,0:T(8,128)S(1)}, u32[]{:S(2)}, u32[]{:S(2)}) async-start(f32[16,8,256]{2,1,0:T(8,128)} %shard_map.149), calls=%async_computation.1 | async-start | bytes 262144 | tf_op jit(solution)/shard_map/all_to_all | solution.py:523
  27.5 0.0 copy-done.2
  27.5 0.0 copy-done.3
  27.5 0.0 copy-start.1
  27.6 6.7 %shard_map.147 = (bf16[2048,512]{1,0:T(8,128)(2,1)S(1)}, f32[384,512]{1,0:T(8,128)S(1)}) custom-call(bf16[2048,512]{1,0:T(8,128)(2,1)} %gr_hbm.3, f32[16,512]{1,0:T(8,128)S(1)} %bitcast.12, f32[16,512]{1,0:T(8,128)S(1)} %bitcast.14, f32[1,512]{1,0:T(1,128)S(1)} %bitcast.16, bf16[512,256]{1,0:T(8,128)(2,1)} %constant.17.clone.fwd_hbm, ...), custom_call_target="tpu_custom_call" | custom-call | flops 2147483648 | bytes 6291456 | tf_op jit(solution)/shard_map/pallas_call | solution.py:452
  34.3 1.1 %all-to-all-done.1 = f32[16,8,256]{2,1,0:T(8,128)S(1)} async-done(((f32[16,8,256]{2,1,0:T(8,128)}), f32[16,8,256]{2,1,0:T(8,128)S(1)}, u32[]{:S(2)}, u32[]{:S(2)}) %all-to-all-start.1) | async-done | bytes 131104 | tf_op jit(solution)/shard_map/all_to_all | solution.py:523
  35.4 0.0 copy-done.1
  35.4 2.2 %shard_map.150 = (bf16[2048,512]{1,0:T(8,128)(2,1)}, f32[16,512]{1,0:T(8,128)}, f32[16,512]{1,0:T(8,128)}, f32[1,512]{1,0:T(1,128)}) custom-call(bf16[2048,512]{1,0:T(8,128)(2,1)S(1)} %get-tuple-element.12.near_ref, f32[128,256]{1,0:T(8,128)S(1)} %bitcast.8, f32[384,512]{1,0:T(8,128)S(1)} %get-tuple-element.14.weighted_ref, ...), custom_call_target="tpu_custom_call" | custom-call | tf_op jit(solution)/shard_map/pallas_call | solution.py:488
Async XLA Ops:
  0.6 22.5 %copy-start = (f32[512,16]{0,1:T(8,128)S(1)}, f32[512,16]{0,1:T(8,128)}, u32[]{:S(2)}) copy-start(f32[512,16]{0,1:T(8,128)} %param.15) | copy-start | bytes 98308
  0.6 26.9 %copy-start.2 = (f32[512,16]{0,1:T(8,128)S(1)}, f32[512,16]{0,1:T(8,128)}, u32[]{:S(2)}) copy-start(f32[512,16]{0,1:T(8,128)} %param.14) | copy-start | bytes 98308
  0.7 26.9 %copy-start.3 = (f32[512]{0:T(512)S(1)}, f32[512]{0:T(512)}, u32[]{:S(2)}) copy-start(f32[512]{0:T(512)} %param.16) | copy-start | bytes 6148
  23.9 11.4 %all-to-all-start.1 = ((f32[16,8,256]{2,1,0:T(8,128)}), f32[16,8,256]{2,1,0:T(8,128)S(1)}, u32[]{:S(2)}, u32[]{:S(2)}) async-start(f32[16,8,256]{2,1,0:T(8,128)} %shard_map.149), calls=%async_computation.1 | async-start | bytes 262144 | tf_op jit(solution)/shard_map/all_to_all | solution.py:523
  27.5 7.8 %copy-start.1 = (bf16[256,72]{1,0:T(8,128)(2,1)S(1)}, bf16[256,72]{1,0:T(8,128)(2,1)}, u32[]{:S(2)}) copy-start(bf16[256,72]{1,0:T(8,128)(2,1)} %constant.20.clone.spread_ref) | copy-start | bytes 110596

commit v5 on v4

--- a/solution.py
+++ b/solution.py
@@ -110,8 +110,14 @@
     rate_copy.wait()
     rates = jnp.exp(rate_ref[...])
     step_decay = jnp.exp(rates * (-float(BLK)))
-    for n in range(NODES):
-        mode_exp[pl.ds(n * MODES, MODES), :] = jnp.exp(rates * (-nodes[n]))
+
+    def decays(low, high):
+        def emit():
+            for n in range(low, high):
+                mode_exp[n * MODES:(n + 1) * MODES, :] = jnp.exp(rates * (-nodes[n]))
+
+        return emit
+
 
     def lanes(c):
         return slice(c * TILE, (c + 1) * TILE)
@@ -209,7 +215,7 @@
         return work
 
     groups = SCHEDULE
-    work = []
+    work = [decays(n, n + 3) for n in range(0, NODES, 3)]
     for group in groups:
         products = []
         for b in group:

time: 37.8 us -> 37.7 us (level)
  no operation moved by 1% of the time
where the time goes in v5:
time: 37.7 us; the launch traced here: 37.4 us
  Pallas kernels  17.3 us (46%)
  blocking collectives  14.8 us (39%)
  starting transfers between devices  3.6 us (10%)
  waiting for transfers between devices  1.06 us (3%)
  between operations  0.71 us (2%)
    all_to_all x1, blocking collectives, on_device(): lax.all_to_all(summed.reshape(MODES, 2 * ROWS, channels // 2), 'ctx', spl...  14.8 us
    pallas_call x1, Pallas kernels, call_sums(): pl.pallas_call(functools.partial(sums_kernel, t['nodes'], blocks), in_spe...  7.62 us
    pallas_call x1, Pallas kernels, call_nearby(): pl.pallas_call(functools.partial(nearby_kernel, t['nodes'], blocks), in_s...  6.74 us
    all_to_all x1, starting transfers between devices, on_device(): lax.all_to_all(scanned, 'ctx', split_axis=0, concat_axis=0, tiled=True)  3.6 us
    pallas_call x1, Pallas kernels, call_finish(): pl.pallas_call(functools.partial(finish_kernel, blocks, scaling), in_spec...  2.17 us
    all_to_all x1, waiting for transfers between devices, on_device(): lax.all_to_all(scanned, 'ctx', split_axis=0, concat_axis=0, tiled=True)  1.06 us
    pallas_call x1, Pallas kernels, call_scan(): pl.pallas_call(functools.partial(scan_kernel, shards, float(tokens)), out...  0.78 us
  transfers between devices with their start and end apart: 1, of which 1 were waited for; matrix products, arithmetic and copies ran while one was open for 0% of the time, Pallas kernels for 18%

profile of v5, /device:TPU:0, one launch (start us, length us, event | category | flops | bytes accessed | tf_op | source)
XLA Modules:
  0.0 37.4 jit_solution(14579960729252224555)
XLA Ops:
  0.6 0.0 copy-start
  0.6 0.0 copy-start.2
  0.7 0.0 copy-start.3
  0.7 7.6 %shard_map.148 = (bf16[256,256]{1,0:T(8,128)(2,1)S(1)}, f32[128,512]{1,0:T(8,128)S(1)}) custom-call(bf16[2048,512]{1,0:T(8,128)(2,1)} %in_hbm.1, bf16[2048,512]{1,0:T(8,128)(2,1)} %gr_hbm.3, f32[16,512]{1,0:T(8,128)} %bitcast.10, bf16[560,256]{1,0:T(8,128)(2,1)} %constant.14.clone.tin_hbm, bf16[560,256]{1,0:T(8,128)(2,1)} %constant.15.clone.tgr_hbm, ...), custom_call_target="tpu_custom_call" | custom-call | flops 2348810240 | bytes 8388608 | tf_op jit(solution)/shard_map/pallas_call | solution.py:421
  8.3 14.8 %all_to_all.10.in_ref = bf16[16,16,256]{2,1,0:T(8,128)(2,1)S(1)} all-to-all(bf16[16,16,256]{2,1,0:T(8,128)(2,1)S(1)} %bitcast.9), channel_id=1, replica_groups=mesh['ctx'=16,'ch'=8] {'ctx'}, dimensions={0} | all-to-all | bytes 262144 | tf_op jit(solution)/shard_map/all_to_all | solution.py:524
  23.0 0.0 copy-done
  23.0 0.8 %shard_map.149 = f32[16,8,256]{2,1,0:T(8,128)} custom-call(bf16[16,16,256]{2,1,0:T(8,128)(2,1)S(1)} %all_to_all.10.in_ref, f32[16,512]{1,0:T(8,128)S(1)} %bitcast.11), custom_call_target="tpu_custom_call" | custom-call | tf_op jit(solution)/shard_map/pallas_call | solution.py:481
  23.8 3.6 %all-to-all-start.1 = ((f32[16,8,256]{2,1,0:T(8,128)}), f32[16,8,256]{2,1,0:T(8,128)S(1)}, u32[]{:S(2)}, u32[]{:S(2)}) async-start(f32[16,8,256]{2,1,0:T(8,128)} %shard_map.149), calls=%async_computation.1 | async-start | bytes 262144 | tf_op jit(solution)/shard_map/all_to_all | solution.py:529
  27.4 0.0 copy-done.2
  27.4 0.0 copy-done.3
  27.5 0.0 copy-start.1
  27.5 6.7 %shard_map.147 = (bf16[2048,512]{1,0:T(8,128)(2,1)S(1)}, f32[384,512]{1,0:T(8,128)S(1)}) custom-call(bf16[2048,512]{1,0:T(8,128)(2,1)} %gr_hbm.3, f32[16,512]{1,0:T(8,128)S(1)} %bitcast.12, f32[16,512]{1,0:T(8,128)S(1)} %bitcast.14, f32[1,512]{1,0:T(1,128)S(1)} %bitcast.16, bf16[512,256]{1,0:T(8,128)(2,1)} %constant.17.clone.fwd_hbm, ...), custom_call_target="tpu_custom_call" | custom-call | flops 2147483648 | bytes 6291456 | tf_op jit(solution)/shard_map/pallas_call | solution.py:458
  34.2 1.1 %all-to-all-done.1 = f32[16,8,256]{2,1,0:T(8,128)S(1)} async-done(((f32[16,8,256]{2,1,0:T(8,128)}), f32[16,8,256]{2,1,0:T(8,128)S(1)}, u32[]{:S(2)}, u32[]{:S(2)}) %all-to-all-start.1) | async-done | bytes 131104 | tf_op jit(solution)/shard_map/all_to_all | solution.py:529
  35.3 0.0 copy-done.1
  35.3 2.2 %shard_map.150 = (bf16[2048,512]{1,0:T(8,128)(2,1)}, f32[16,512]{1,0:T(8,128)}, f32[16,512]{1,0:T(8,128)}, f32[1,512]{1,0:T(1,128)}) custom-call(bf16[2048,512]{1,0:T(8,128)(2,1)S(1)} %get-tuple-element.12.near_ref, f32[128,256]{1,0:T(8,128)S(1)} %bitcast.8, f32[384,512]{1,0:T(8,128)S(1)} %get-tuple-element.14.weighted_ref, ...), custom_call_target="tpu_custom_call" | custom-call | tf_op jit(solution)/shard_map/pallas_call | solution.py:494
Async XLA Ops:
  0.6 22.4 %copy-start = (f32[512,16]{0,1:T(8,128)S(1)}, f32[512,16]{0,1:T(8,128)}, u32[]{:S(2)}) copy-start(f32[512,16]{0,1:T(8,128)} %param.15) | copy-start | bytes 98308
  0.6 26.8 %copy-start.2 = (f32[512,16]{0,1:T(8,128)S(1)}, f32[512,16]{0,1:T(8,128)}, u32[]{:S(2)}) copy-start(f32[512,16]{0,1:T(8,128)} %param.14) | copy-start | bytes 98308
  0.7 26.8 %copy-start.3 = (f32[512]{0:T(512)S(1)}, f32[512]{0:T(512)}, u32[]{:S(2)}) copy-start(f32[512]{0:T(512)} %param.16) | copy-start | bytes 6148
  23.8 11.4 %all-to-all-start.1 = ((f32[16,8,256]{2,1,0:T(8,128)}), f32[16,8,256]{2,1,0:T(8,128)S(1)}, u32[]{:S(2)}, u32[]{:S(2)}) async-start(f32[16,8,256]{2,1,0:T(8,128)} %shard_map.149), calls=%async_computation.1 | async-start | bytes 262144 | tf_op jit(solution)/shard_map/all_to_all | solution.py:529
  27.5 7.8 %copy-start.1 = (bf16[256,72]{1,0:T(8,128)(2,1)S(1)}, bf16[256,72]{1,0:T(8,128)(2,1)}, u32[]{:S(2)}) copy-start(bf16[256,72]{1,0:T(8,128)(2,1)} %constant.20.clone.spread_ref) | copy-start | bytes 110596
